TPU v7x, 32 devices: a whole 2x2x4 slice. The times are simulated.
32 devices in a mesh: group: 2 (over y), attn: 4 (over z), sect: 2 (over x), pair: 2 (over core).
Axes of the slice: x: 2, y: 2, z: 4, core: 2. Of those that a mesh axis runs over, the one named last changes fastest.
Arguments:
- queries: bfloat16 [512, 4096], P(('group', 'attn'), ('sect', 'pair')), parts along dimension 0, may hold values from -200 to 200
- kv_pool: bfloat16 [4, 8, 128, 256], P('sect', ('group', 'attn')), parts along dimension 1, may hold values from -8 to 8
- block_list: int32 [8, 2], P(('group', 'attn')), parts along dimension 0, may hold values from 0 to 3, as said below
- cache_len: int32 [8], P(('group', 'attn')), parts along dimension 0, may hold values from 128 to 256, as said below
- out_weight: bfloat16 [4096, 2048], P(('sect', 'pair'), 'attn'), may hold values from -0.09375 to 0.09375
- residual: bfloat16 [512, 2048], P(('group', 'attn', 'sect', 'pair')), parts along dimension 0, may hold values from -4 to 4
- norm_gain: float32 [2048], replicated, may hold values from 0.1 to 1.9
- router: bfloat16 [2048, 8], replicated, may hold values from -50 to 50
- expert_ids: int32 [512, 4], P(('group', 'attn', 'sect', 'pair')), parts along dimension 0, may hold values from 0 to 7, all different within a row; in each aligned block of 16 rows (0 to 15, 16 to 31, ...) at most 16 rows name the same one
- w_gate: bfloat16 [8, 2048, 768], P(('attn', 'pair'), None, 'sect'), may hold values from -0.125 to 0.125
- w_up: bfloat16 [8, 2048, 768], P(('attn', 'pair'), None, 'sect'), may hold values from -0.125 to 0.125
- w_down: bfloat16 [8, 768, 2048], P(('attn', 'pair'), None, 'sect'), may hold values from -0.21875 to 0.21875
Outputs:
- layer_out: bfloat16 [512, 2048], P(('group', 'attn', 'sect', 'pair')), parts along dimension 0
There are 2 independent parts, one for each index of `group`. A program takes and returns all parts, laid end to end along the dimension named above; an argument that names none is the same for every part. Nothing has to cross between parts.
Inputs may be any that keep to these rules, and one draw needn't show every extreme that they name: `block_list`: A group's 2 blocks are distinct, and every block of the pool is listed by some group. `cache_len`: some group has 256 live positions and some group 128. `expert_ids`: each row names 4 different experts; among the rows of one device no expert is named by more than 16 rows, a bound that some block reaches.
All inputs are finite; a program needn't handle non-finite values.
Results may differ from a plain program's by a relative error of at most 0.013.
Values may be sent and summed in bfloat16 or wider, within the bound.
A program may use at most 64 MiB of HBM per device.

v0:
```python
import math

import jax
import jax.numpy as jnp
from jax import lax
from jax.sharding import PartitionSpec as P

HEADS = 32
KV_HEADS = 4
HEAD_DIM = 128


def on_device(
    queries,
    kv_pool,
    block_list,
    cache_len,
    out_weight,
    residual,
    norm_gain,
    router,
    expert_ids,
    w_gate,
    w_up,
    w_down,
):
    head_dim = HEAD_DIM
    per_kv = HEADS // KV_HEADS
    group_rows, head_cols = queries.shape
    local_heads = head_cols // head_dim
    pool_all = lax.all_gather(kv_pool, "attn", axis=1, tiled=True)
    picked = jnp.take(pool_all, block_list[0], axis=1)
    kv_local = lax.axis_index("pair") * local_heads // per_kv
    chosen = lax.dynamic_index_in_dim(picked, kv_local, 0, keepdims=False)
    chosen = chosen.reshape(-1, 2 * head_dim)
    key_rows = chosen[:, :head_dim]
    values = chosen[:, head_dim:]
    query_heads = queries.reshape(group_rows, local_heads, head_dim)
    scores = jnp.einsum(
        "rhd,td->rht", query_heads, key_rows, preferred_element_type=jnp.float32
    ) / math.sqrt(head_dim)
    live_mask = jnp.arange(key_rows.shape[0]) < cache_len[0]
    scores = jnp.where(live_mask, scores, -jnp.inf)
    row_top = jnp.max(scores, axis=-1, keepdims=True)
    lifted = jnp.exp(scores - row_top)
    row_total = jnp.sum(lifted, axis=-1)
    soft_weights = lifted.astype(jnp.bfloat16)
    mixed_heads = (
        jnp.einsum("rht,td->rhd", soft_weights, values, preferred_element_type=jnp.float32)
        / row_total[..., None]
    )
    attended = mixed_heads.reshape(group_rows, head_cols).astype(jnp.bfloat16)
    partial_value = jnp.dot(
        attended,
        lax.all_gather(out_weight, "attn", axis=1, tiled=True),
        preferred_element_type=jnp.float32,
    )
    summed = lax.psum_scatter(partial_value, ("sect", "pair"), scatter_dimension=0, tiled=True)
    mixed_f32 = residual.astype(jnp.float32) + summed
    mixed_rows = mixed_f32.astype(jnp.bfloat16)
    mixed_f32 = mixed_rows.astype(jnp.float32)
    normed = (
        mixed_f32
        * lax.rsqrt(jnp.mean(mixed_f32 * mixed_f32, axis=-1, keepdims=True) + 1e-06)
        * norm_gain
    ).astype(jnp.bfloat16)
    logits = jnp.dot(normed, router, preferred_element_type=jnp.float32)
    chosen_logits = jnp.take_along_axis(logits, expert_ids, axis=1)
    route_weights = jax.nn.softmax(chosen_logits, axis=-1)
    row_count, top_count = expert_ids.shape
    expert_count = router.shape[1]
    model_width = residual.shape[1]
    capacity = max(2, row_count * top_count // expert_count * 2)
    flat_ids = expert_ids.reshape(-1)
    onehot = (flat_ids[:, None] == jnp.arange(expert_count, dtype=jnp.int32)[None, :]).astype(
        jnp.int32
    )
    earlier = jnp.cumsum(onehot, axis=0) - onehot
    slot_index = jnp.sum(earlier * onehot, axis=1)
    source = jnp.repeat(jnp.arange(row_count, dtype=jnp.int32), top_count)
    outgoing = (
        jnp.zeros((expert_count, capacity, model_width), jnp.bfloat16)
        .at[flat_ids, slot_index]
        .set(normed[source])
    )
    received = lax.all_to_all(outgoing, ("attn", "pair"), split_axis=0, concat_axis=0, tiled=True)
    sections = lax.axis_size("sect")
    every_section = lax.all_gather(received, "sect", axis=0, tiled=True)
    tokens_in = every_section.reshape(-1, model_width)
    gate_val = jnp.dot(tokens_in, w_gate[0], preferred_element_type=jnp.float32)
    up_val = jnp.dot(tokens_in, w_up[0], preferred_element_type=jnp.float32)
    part_hidden = (jax.nn.silu(gate_val) * up_val).astype(jnp.bfloat16)
    hidden = lax.all_gather(part_hidden, "sect", axis=1, tiled=True)
    out_slice = jnp.dot(hidden, w_down[0], preferred_element_type=jnp.float32).astype(jnp.bfloat16)
    out_slice = out_slice.reshape(sections, expert_count, capacity, model_width // sections)
    segmented = lax.all_to_all(out_slice, "sect", split_axis=0, concat_axis=3, tiled=True)
    returned = lax.all_to_all(
        segmented[0], ("attn", "pair"), split_axis=0, concat_axis=0, tiled=True
    )
    gathered = (
        returned[flat_ids, slot_index]
        .reshape(row_count, top_count, model_width)
        .astype(jnp.float32)
    )
    joined = jnp.sum(route_weights[:, :, None] * gathered, axis=1)
    return (mixed_f32 + joined).astype(jnp.bfloat16)


def solution(mesh):
    placed = (
        P(("group", "attn"), ("sect", "pair")),
        P("sect", ("group", "attn"), None, None),
        P(("group", "attn"), None),
        P(("group", "attn")),
        P(("sect", "pair"), "attn"),
        P(("group", "attn", "sect", "pair"), None),
        P(),
        P(),
        P(("group", "attn", "sect", "pair"), None),
        P(("attn", "pair"), None, "sect"),
        P(("attn", "pair"), None, "sect"),
        P(("attn", "pair"), None, "sect"),
    )
    return jax.shard_map(
        on_device,
        mesh=mesh,
        in_specs=placed,
        out_specs=P(("group", "attn", "sect", "pair"), None),
        check_vma=False,
    )
```

profile of v0, /device:TPU:0, one launch (start us, length us, event | category | flops | bytes accessed | tf_op | source)
XLA Modules:
  0.0 218.1 jit_solution(17253515599728058763)
XLA Ops:
  6.5 0.7 all-gather.3.cloned.1.call-update
  7.3 0.0 reduce-scatter.2.cloned.1.call-start
  8.0 0.7 fusion.37
  8.6 20.4 %all_gather.12 = bf16[2,4,128,256]{3,2,1,0:T(8,128)(2,1)S(1)} all-gather(bf16[2,1,128,256]{3,2,1,0:T(8,128)(2,1)} %param.13), channel_id=1, replica_groups=mesh['group'=2,'attn'=4,'sect'=2,'pair'=2] {'attn'}, dimensions={1}, use_global_device_ids=true | all-gather | bytes 655360 | tf_op jit(solution)/shard_map/all_gather | solution.py:31
  29.0 0.6 gather_fusion
  29.6 0.1 dynamic-slice_select_fusion
  29.7 0.4 fusion.47
  30.1 0.1 copy.35
  30.2 0.3 fusion.20
  30.5 63.6 %all-gather.3.cloned.1.call-done = bf16[1024,2048]{1,0:T(8,128)(2,1)} async-done(((bf16[1024,512]{1,0:T(8,128)(2,1)}), bf16[1024,2048]{1,0:T(8,128)(2,1)}) %all-gather.3.cloned.1.call-update) | async-done | bytes 4194320 | tf_op jit(solution)/shard_map/all_gather | solution.py:55
  94.1 3.9 %fusion.26 = f32[64,2048]{1,0:T(8,128)} fusion(bf16[1024,2048]{1,0:T(8,128)(2,1)} %all-gather.3.cloned.1.call-done, bf16[8,8,8,128]{3,2,1,0:T(8,128)(2,1)S(1)} %bitcast.94), kind=kOutput, calls=%fused_computation.31 | convolution fusion | flops 268435456 | bytes 4849664 | tf_op jit(solution)/shard_map/dot_general | solution.py:53
  98.0 0.0 all-gather.5.cloned.1.call-start
  98.1 0.1 copy.36
  98.2 0.1 eq.15
  98.3 0.1 reshape.172
  98.4 0.1 reshape.173
  98.4 0.1 fusion.33
  98.5 0.1 reduce_window_sum.11
  98.6 0.2 select_reduce_fusion
  98.8 19.7 %reduce-scatter.2.cloned.1.call-done = f32[16,2048]{1,0:T(8,128)} async-done(((f32[64,2048]{1,0:T(8,128)}), f32[16,2048]{1,0:T(8,128)}) %reduce-scatter.2.cloned.1.call-update) | async-done | bytes 131088 | tf_op jit(solution)/shard_map/reduce_scatter | solution.py:58
  118.6 1.0 fusion.22
  119.6 0.1 fusion.24
  119.7 0.7 gather_fusion.1
  120.5 6.4 %scatter_fusion = bf16[8,16,2048]{2,1,0:T(8,128)(2,1)S(1)} fusion(bf16[8,16,2048]{2,1,0:T(8,128)(2,1)S(1)} %broadcast_in_dim.46, s32[64]{0:T(128)S(1)} %get-tuple-element.7, bf16[64,2048]{1,0:T(8,128)(2,1)S(1)} %gather_fusion.1), kind=kCustom, calls=%fused_computation.4 | custom fusion | bytes 786944 | tf_op jit(solution)/shard_map/scatter | solution.py:84
  126.9 19.9 %all_to_all.25 = bf16[8,16,2048]{2,1,0:T(8,128)(2,1)} all-to-all(bf16[8,16,2048]{2,1,0:T(8,128)(2,1)S(1)} %scatter_fusion), channel_id=1, replica_groups=mesh['group'=2,'attn'=4,'sect'=2,'pair'=2] {'attn','pair'}, dimensions={0} | all-to-all | bytes 1048576 | tf_op jit(solution)/shard_map/all_to_all | solution.py:86
  146.8 19.4 %all-gather.5.cloned.1.call-done = bf16[16,16,2048]{2,1,0:T(8,128)(2,1)} async-done(((bf16[8,16,2048]{2,1,0:T(8,128)(2,1)}), bf16[16,16,2048]{2,1,0:T(8,128)(2,1)}) %all-gather.5.cloned.1.call-update) | async-done | bytes 1048592 | tf_op jit(solution)/shard_map/all_gather | solution.py:88
  166.2 2.5 %fusion.5 = f32[256,384]{1,0:T(8,128)S(1)} fusion(bf16[256,2048]{1,0:T(8,128)(2,1)} %bitcast.92, bf16[1,2048,384]{2,1,0:T(8,128)(2,1)} %param.21), kind=kOutput, calls=%fused_computation.10 | convolution fusion | flops 402653184 | bytes 3014656 | tf_op jit(solution)/shard_map/dot_general | solution.py:90
  168.7 0.7 fusion.17
  169.4 7.3 %all_gather.15 = bf16[256,768]{1,0:T(8,128)(2,1)S(1)} all-gather(bf16[256,384]{1,0:T(8,128)(2,1)S(1)} %fusion.17), channel_id=1, replica_groups=mesh['group'=2,'attn'=4,'sect'=2,'pair'=2] {'sect'}, dimensions={1}, use_global_device_ids=true | all-gather | bytes 589824 | tf_op jit(solution)/shard_map/all_gather | solution.py:93
  176.8 0.6 fusion.7
  177.3 9.8 %all_to_all.26 = bf16[2,8,16,1024]{3,2,1,0:T(8,128)(2,1)S(1)} all-to-all(bf16[2,8,16,1024]{3,2,1,0:T(8,128)(2,1)S(1)} %bitcast.90), channel_id=1, replica_groups=mesh['group'=2,'attn'=4,'sect'=2,'pair'=2] {'sect'}, dimensions={0} | all-to-all | bytes 1048576 | tf_op jit(solution)/shard_map/all_to_all | solution.py:96
  187.1 0.5 copy.43
  187.7 1.2 squeeze.28
  188.9 4.6 %all-to-all-start.2 = ((bf16[8,16,2048]{2,1,0:T(8,128)(2,1)}), bf16[8,16,2048]{2,1,0:T(8,128)(2,1)S(1)}, u32[]{:S(2)}, u32[]{:S(2)}) async-start(bf16[8,16,2048]{2,1,0:T(8,128)(2,1)} %squeeze.28), calls=%async_computation.3 | async-start | bytes 1048576 | tf_op jit(solution)/shard_map/all_to_all | solution.py:97
  193.5 0.1 copy.39
  193.6 0.1 copy.40
  193.7 0.1 reshape.199
  193.8 0.1 fusion.50
  193.9 0.7 gather_fusion.3
  194.6 0.1 reshape.202
  194.7 0.1 fusion.45
  194.8 0.2 fusion.35
  195.0 0.1 fusion.34
  195.1 13.7 %all-to-all-done.2 = bf16[8,16,2048]{2,1,0:T(8,128)(2,1)S(1)} async-done(((bf16[8,16,2048]{2,1,0:T(8,128)(2,1)}), bf16[8,16,2048]{2,1,0:T(8,128)(2,1)S(1)}, u32[]{:S(2)}, u32[]{:S(2)}) %all-to-all-start.2) | async-done | bytes 524320 | tf_op jit(solution)/shard_map/all_to_all | solution.py:97
  208.8 1.5 gather_fusion.2
  210.3 0.2 reshape.176
  210.5 0.4 multiply_reduce_fusion
  210.9 0.7 fusion.25
  (32 shorter events, 0.2 us)
Async XLA Ops:
  6.5 170.2 %copy-start = (bf16[1,768,1024]{2,1,0:T(8,128)(2,1)S(1)}, bf16[1,768,1024]{2,1,0:T(8,128)(2,1)}, u32[]{:S(2)}) copy-start(bf16[1,768,1024]{2,1,0:T(8,128)(2,1)} %param.23) | copy-start | bytes 4718596
  6.5 23.1 %copy-start.8 = (s32[1,2]{1,0:T(1,128)S(1)}, s32[1,2]{1,0:T(1,128)}, u32[]{:S(2)}) copy-start(s32[1,2]{1,0:T(1,128)} %param.14) | copy-start | bytes 28
  6.5 23.2 %copy-start.7 = (bf16[64,1024]{1,0:T(8,128)(2,1)S(1)}, bf16[64,1024]{1,0:T(8,128)(2,1)}, u32[]{:S(2)}) copy-start(bf16[64,1024]{1,0:T(8,128)(2,1)} %param.12) | copy-start | bytes 393220
  6.5 87.6 %all-gather.3.cloned.1.call-start = ((), (), s32[]{:S(2)}) async-start(), calls=%async_computation.4 | async-start | bytes 5242880 | tf_op jit(solution)/shard_map/all_gather | solution.py:55
  7.3 111.3 %reduce-scatter.2.cloned.1.call-start = ((), (), s32[]{:S(2)}) async-start(), calls=%async_computation.5 | async-start | bytes 655360 | tf_op jit(solution)/shard_map/reduce_scatter | solution.py:58
  94.1 3.9 %copy-start.5 = (s32[16,4]{0,1:T(4,128)S(1)}, s32[16,4]{0,1:T(4,128)}, u32[]{:S(2)}) copy-start(s32[16,4]{0,1:T(4,128)} %param.20) | copy-start | bytes 772
  94.1 24.4 %copy-start.2 = (bf16[16,2048]{1,0:T(8,128)(2,1)S(1)}, bf16[16,2048]{1,0:T(8,128)(2,1)}, u32[]{:S(2)}) copy-start(bf16[16,2048]{1,0:T(8,128)(2,1)} %param.17) | copy-start | bytes 196612
  94.1 25.5 %copy-start.4 = (f32[2048]{0:T(1024)S(1)}, f32[2048]{0:T(1024)}, u32[]{:S(2)}) copy-start(f32[2048]{0:T(1024)} %param.18) | copy-start | bytes 24580
  98.0 68.1 %all-gather.5.cloned.1.call-start = ((), (), s32[]{:S(2)}) async-start(), calls=%async_computation.6 | async-start | bytes 1572864 | tf_op jit(solution)/shard_map/all_gather | solution.py:88
  146.8 21.9 %copy-start.6 = (bf16[1,2048,384]{2,1,0:T(8,128)(2,1)S(1)}, bf16[1,2048,384]{2,1,0:T(8,128)(2,1)}, u32[]{:S(2)}) copy-start(bf16[1,2048,384]{2,1,0:T(8,128)(2,1)} %param.22) | copy-start | bytes 4718596
  166.2 2.5 %copy-start.1 = (bf16[16,16,2048]{2,1,0:T(8,128)(2,1)S(1)}, bf16[16,16,2048]{2,1,0:T(8,128)(2,1)}, u32[]{:S(2)}) copy-start(bf16[16,16,2048]{2,1,0:T(8,128)(2,1)} %all-gather.5.cloned.1.call-done) | copy-start | bytes 3145732
  187.1 6.6 %copy-start.3 = (bf16[2048,8]{0,1:T(8,128)(2,1)S(1)}, bf16[2048,8]{0,1:T(8,128)(2,1)}, u32[]{:S(2)}) copy-start(bf16[2048,8]{0,1:T(8,128)(2,1)} %param.19) | copy-start | bytes 98308
  188.9 20.0 %all-to-all-start.2 = ((bf16[8,16,2048]{2,1,0:T(8,128)(2,1)}), bf16[8,16,2048]{2,1,0:T(8,128)(2,1)S(1)}, u32[]{:S(2)}, u32[]{:S(2)}) async-start(bf16[8,16,2048]{2,1,0:T(8,128)(2,1)} %squeeze.28), calls=%async_computation.3 | async-start | bytes 1048576 | tf_op jit(solution)/shard_map/all_to_all | solution.py:97
Sparse Core Ops, SparseCore 0:
  8.9 85.1 all-gather.2
  98.1 20.3 reduce-scatter.1
  146.9 19.2 all-gather.4
where the time goes:
time: 218 us
  waiting for transfers between devices  117 us (54%)
  blocking collectives  57.4 us (26%)
  between operations  14 us (6%)
  local copies, waits for them, and re-layouts  12.6 us (6%)
  matrix products  8.49 us (4%)
  starting transfers between devices  4.68 us (2%)
  other arithmetic  3.71 us (2%)
    all_gather x1, waiting for transfers between devices, on_device(): lax.all_gather(out_weight, 'attn', axis=1, tiled=True)  63.6 us
    all_gather x1, blocking collectives, on_device(): pool_all = lax.all_gather(kv_pool, 'attn', axis=1, tiled=True)  20.4 us
    all_to_all x1, blocking collectives, on_device(): lax.all_to_all(outgoing, ('attn', 'pair'), split_axis=0, concat_axis=0, t...  19.9 us
    reduce_scatter x1, waiting for transfers between devices, on_device(): lax.psum_scatter(partial_value, ('sect', 'pair'), scatter_dimension=0, ti...  19.7 us
    all_gather x1, waiting for transfers between devices, on_device(): every_section = lax.all_gather(received, 'sect', axis=0, tiled=True)  19.4 us
    all_to_all x1, waiting for transfers between devices, on_device(): lax.all_to_all(segmented[0], ('attn', 'pair'), split_axis=0, concat_axis=...  13.7 us
    all_to_all x1, blocking collectives, on_device(): lax.all_to_all(out_slice, 'sect', split_axis=0, concat_axis=3, tiled=True)  9.79 us
    all_gather x1, blocking collectives, on_device(): hidden = lax.all_gather(part_hidden, 'sect', axis=1, tiled=True)  7.32 us
  transfers between devices with their start and end apart: 4, of which 4 were waited for; matrix products, arithmetic and copies ran while one was open for 2% of the time, Pallas kernels for 0%

commit v1 on v0

--- a/solution.py
+++ b/solution.py
@@ -1,8 +1,11 @@
+import functools
 import math
 
 import jax
 import jax.numpy as jnp
 from jax import lax
+from jax.experimental import pallas as pl
+from jax.experimental.pallas import tpu as pltpu
 from jax.sharding import PartitionSpec as P
 
 HEADS = 32
@@ -10,7 +13,7 @@
 HEAD_DIM = 128
 
 
-def on_device(
+def by_collectives(
     queries,
     kv_pool,
     block_list,
@@ -106,6 +109,540 @@
     return (mixed_f32 + joined).astype(jnp.bfloat16)
 
 
+MESH = pl.DeviceIdType.MESH
+LANES = 128
+VMEM_BYTES = 48 * 1024 * 1024
+BF16 = jnp.bfloat16
+F32 = jnp.float32
+
+
+def layer_kernel(
+    sizes,
+    q_ref,
+    kv_ref,
+    list_ref,
+    len_ref,
+    res_ref,
+    gain_ref,
+    router_ref,
+    ids_ref,
+    wo_hbm,
+    wg_hbm,
+    wu_hbm,
+    wd_hbm,
+    out_ref,
+    wo,
+    wg,
+    wu,
+    wd,
+    kvbuf,
+    att,
+    part_f32,
+    part,
+    rs_in,
+    sum_out,
+    mix_in,
+    mix_f32,
+    router_pad,
+    rows,
+    hid,
+    prod_f32,
+    prod,
+    pair_in,
+    ret_out,
+    ret_in,
+    tot_f32,
+    tot,
+    fin_in,
+    fin_f32,
+    w_sem,
+    kv_s,
+    kv_r,
+    att_s,
+    att_r,
+    rs_s,
+    rs_r,
+    mix_s,
+    mix_r,
+    nz_s,
+    nz_r,
+    nx_s,
+    nx_r,
+    nc_s,
+    nc_r,
+    hid_s,
+    hid_r,
+    pair_s,
+    pair_r,
+    ret_s,
+    ret_r,
+    fin_s,
+    fin_r,
+):
+    n_attn, n_sect, n_pair = sizes
+    quarters = n_sect * n_pair
+    z = lax.axis_index("attn")
+    x = lax.axis_index("sect")
+    c = lax.axis_index("pair")
+    quarter = x * n_pair + c
+    own = res_ref.shape[0]
+    width = res_ref.shape[1]
+    group_rows, head_cols = q_ref.shape
+    local_heads = head_cols // HEAD_DIM
+    kv_local = c * local_heads // (HEADS // KV_HEADS)
+    blocks = kv_ref.shape[1]
+    sends = []
+
+    def send(src, dst, s_sem, r_sem, **where):
+        copy = pltpu.make_async_remote_copy(
+            src_ref=src,
+            dst_ref=dst,
+            send_sem=s_sem,
+            recv_sem=r_sem,
+            device_id=where,
+            device_id_type=MESH,
+        )
+        copy.start()
+        sends.append(copy)
+        return copy
+
+    loads = [
+        pltpu.make_async_copy(src, dst, w_sem.at[i])
+        for i, (src, dst) in enumerate(
+            ((wo_hbm, wo), (wg_hbm.at[0], wg), (wu_hbm.at[0], wu), (wd_hbm.at[0], wd))
+        )
+    ]
+    for load in loads:
+        load.start()
+
+    barrier = pltpu.get_barrier_semaphore()
+    for dz in range(n_attn):
+        for dx in range(n_sect):
+            for dc in range(n_pair):
+                if dz + dx + dc:
+                    pl.semaphore_signal(
+                        barrier,
+                        inc=1,
+                        device_id={
+                            "attn": lax.rem(z + dz, n_attn),
+                            "sect": lax.rem(x + dx, n_sect),
+                            "pair": lax.rem(c + dc, n_pair),
+                        },
+                        device_id_type=MESH,
+                    )
+    pl.semaphore_wait(barrier, n_attn * quarters - 1)
+
+    def ahead(d):
+        return lax.rem(z + d, n_attn)
+
+    def behind(d):
+        return lax.rem(z + (n_attn - d), n_attn)
+
+    kv_slot = pl.ds(z * blocks, blocks)
+    kv_copies = [
+        send(
+            kv_ref.at[kv_local],
+            kvbuf.at[kv_slot],
+            kv_s.at[d - 1],
+            kv_r.at[d - 1],
+            attn=ahead(d),
+        )
+        for d in range(1, n_attn)
+    ]
+    kvbuf[kv_slot] = kv_ref[kv_local]
+    router_pad[...] = jnp.zeros_like(router_pad)
+    router_pad[:, : router_ref.shape[1]] = router_ref[...]
+    for copy in kv_copies:
+        copy.wait_recv()
+
+    listed = list_ref.shape[1]
+    picked = [kvbuf[list_ref[0, j]] for j in range(listed)]
+    cache = jnp.concatenate(picked, axis=0)
+    keys = cache[:, :HEAD_DIM]
+    values = cache[:, HEAD_DIM:]
+    heads = jnp.concatenate(
+        [q_ref[:, h * HEAD_DIM : (h + 1) * HEAD_DIM] for h in range(local_heads)], axis=0
+    )
+    scores = lax.dot_general(
+        heads, keys, (((1,), (1,)), ((), ())), preferred_element_type=F32
+    ) / math.sqrt(HEAD_DIM)
+    place = lax.broadcasted_iota(jnp.int32, scores.shape, 1)
+    scores = jnp.where(place < len_ref[0], scores, -jnp.inf)
+    lifted = jnp.exp(scores - jnp.max(scores, axis=-1, keepdims=True))
+    row_total = jnp.sum(lifted, axis=-1, keepdims=True)
+    mixed = jnp.dot(lifted.astype(BF16), values, preferred_element_type=F32) / row_total
+    for h in range(local_heads):
+        att[0, :, h * HEAD_DIM : (h + 1) * HEAD_DIM] = mixed[
+            h * group_rows : (h + 1) * group_rows
+        ].astype(BF16)
+    att_copies = [None] + [
+        send(att.at[0], att.at[d], att_s.at[d - 1], att_r.at[d - 1], attn=ahead(d))
+        for d in range(1, n_attn)
+    ]
+
+    def plane(step):
+        return lax.div(step, n_pair), lax.rem(step, n_pair)
+
+    loads[0].wait()
+    rs_copies = []
+    mix_copies = []
+
+    def project(d):
+        if d:
+            att_copies[d].wait_recv()
+        value = jnp.dot(att[d], wo[...], preferred_element_type=F32)
+        value = value.reshape(part_f32.shape[1:])
+        part_f32[d] = value
+        part[d] = value.astype(BF16)
+        copies = []
+        for j in range(1, quarters):
+            to = lax.rem(quarter + j, quarters)
+            to_x, to_c = plane(to)
+            copies.append(
+                send(
+                    part.at[d, to],
+                    rs_in.at[d, j - 1],
+                    rs_s.at[d, j - 1],
+                    rs_r.at[d, j - 1],
+                    sect=to_x,
+                    pair=to_c,
+                )
+            )
+        rs_copies.append(copies)
+
+    def pass_on(d):
+        for copy in rs_copies[d]:
+            copy.wait_recv()
+        total = part_f32[d, quarter]
+        for j in range(quarters - 1):
+            total = total + rs_in[d, j].astype(F32)
+        if d == 0:
+            mix_f32[z] = total
+        else:
+            sum_out[d - 1] = total.astype(BF16)
+            mix_copies.append(
+                send(
+                    sum_out.at[d - 1],
+                    mix_in.at[z],
+                    mix_s.at[d - 1],
+                    mix_r.at[d - 1],
+                    attn=behind(d),
+                )
+            )
+
+    for d in range(n_attn + 1):
+        if d < n_attn:
+            project(d)
+        if d:
+            pass_on(d - 1)
+    for d in range(1, n_attn):
+        mix_copies[d - 1].wait_recv()
+        mix_f32[ahead(d)] = mix_in[ahead(d)].astype(F32)
+
+    span = width // n_attn
+    mixed_f32 = res_ref[...].astype(F32) + jnp.concatenate(
+        [mix_f32[a] for a in range(n_attn)], axis=1
+    )
+    mixed_f32 = mixed_f32.astype(BF16).astype(F32)
+    normed = (
+        mixed_f32
+        * lax.rsqrt(jnp.mean(mixed_f32 * mixed_f32, axis=-1, keepdims=True) + 1e-06)
+        * gain_ref[...]
+    ).astype(BF16)
+    logits = jnp.dot(normed, router_pad[...], preferred_element_type=F32)
+    lane = lax.broadcasted_iota(jnp.int32, logits.shape, 1)
+    chosen = lane == ids_ref[:, 0:1]
+    for k in range(1, ids_ref.shape[1]):
+        chosen = jnp.logical_or(chosen, lane == ids_ref[:, k : k + 1])
+    logits = jnp.where(chosen, logits, -jnp.inf)
+    raised = jnp.exp(logits - jnp.max(logits, axis=-1, keepdims=True))
+    route = raised / jnp.sum(raised, axis=-1, keepdims=True)
+    rows[0, quarter, :, :width] = normed
+    rows[0, quarter, :, width:] = route.astype(BF16)
+
+    nz_copies = [None] + [
+        send(
+            rows.at[0, quarter],
+            rows.at[d, quarter],
+            nz_s.at[d - 1],
+            nz_r.at[d - 1],
+            attn=ahead(d),
+        )
+        for d in range(1, n_attn)
+    ]
+    nx_copies = [None] * n_attn
+    nc_copies = [None] * n_attn
+    for load in loads[1:]:
+        load.wait()
+
+    def to_cores(d, dx):
+        from_q = lax.rem(x + (n_sect - dx), n_sect) * n_pair + c
+        return [
+            send(
+                rows.at[d, from_q],
+                rows.at[d, from_q],
+                nc_s.at[d, dx, dc - 1],
+                nc_r.at[d, dx, dc - 1],
+                pair=lax.rem(c + dc, n_pair),
+            )
+            for dc in range(1, n_pair)
+        ]
+
+    def spread(d):
+        if d:
+            nz_copies[d].wait_recv()
+        nx_copies[d] = [
+            send(
+                rows.at[d, quarter],
+                rows.at[d, quarter],
+                nx_s.at[d, dx - 1],
+                nx_r.at[d, dx - 1],
+                sect=lax.rem(x + dx, n_sect),
+            )
+            for dx in range(1, n_sect)
+        ]
+        nc_copies[d] = to_cores(d, 0)
+
+    def spread_on(d):
+        for dx in range(1, n_sect):
+            nx_copies[d][dx - 1].wait_recv()
+            nc_copies[d] += to_cores(d, dx)
+
+    hid_copies = [None] * n_attn
+    pair_copies = [None] * n_attn
+    ret_copies = [None] * n_attn
+    expert = z * n_pair + c
+
+    def up(d):
+        for copy in nc_copies[d]:
+            copy.wait_recv()
+        tokens = rows[d].reshape(quarters * own, rows.shape[-1])[:, :width]
+        gate_val = jnp.dot(tokens, wg[...], preferred_element_type=F32)
+        up_val = jnp.dot(tokens, wu[...], preferred_element_type=F32)
+        hid[d, x] = (gate_val / (1.0 + jnp.exp(-gate_val)) * up_val).astype(BF16)
+        hid_copies[d] = [
+            send(
+                hid.at[d, x],
+                hid.at[d, x],
+                hid_s.at[d, dx - 1],
+                hid_r.at[d, dx - 1],
+                sect=lax.rem(x + dx, n_sect),
+            )
+            for dx in range(1, n_sect)
+        ]
+
+    def down(d):
+        for copy in hid_copies[d]:
+            copy.wait_recv()
+        hidden = jnp.concatenate([hid[d, i] for i in range(n_sect)], axis=1)
+        value = jnp.dot(hidden, wd[...], preferred_element_type=F32)
+        weights = rows[d].reshape(quarters * own, rows.shape[-1])[:, width:].astype(F32)
+        lanes = lax.broadcasted_iota(jnp.int32, weights.shape, 1)
+        weight = jnp.sum(jnp.where(lanes == expert, weights, 0.0), axis=-1, keepdims=True)
+        value = (value * weight).reshape(n_sect, n_pair, own, value.shape[-1])
+        for i in range(n_sect):
+            for j in range(n_pair):
+                prod_f32[d, j, i] = value[i, j]
+                prod[d, j, i] = value[i, j].astype(BF16)
+        pair_copies[d] = [
+            send(
+                prod.at[d, lax.rem(c + dc, n_pair)],
+                pair_in.at[d, dc - 1],
+                pair_s.at[d, dc - 1],
+                pair_r.at[d, dc - 1],
+                pair=lax.rem(c + dc, n_pair),
+            )
+            for dc in range(1, n_pair)
+        ]
+
+    def give_back(d):
+        for copy in pair_copies[d]:
+            copy.wait_recv()
+        total = prod_f32[d, c]
+        for j in range(n_pair - 1):
+            total = total + pair_in[d, j].astype(F32)
+        if d == 0:
+            tot_f32[...] = total
+        else:
+            ret_out[d - 1] = total.astype(BF16)
+            ret_copies[d] = send(
+                ret_out.at[d - 1],
+                ret_in.at[d - 1],
+                ret_s.at[d - 1],
+                ret_r.at[d - 1],
+                attn=behind(d),
+            )
+
+    spread(0)
+    for d in range(n_attn + 2):
+        if d + 1 < n_attn:
+            spread(d + 1)
+        if d < n_attn:
+            spread_on(d)
+            up(d)
+        if 1 <= d <= n_attn:
+            down(d - 1)
+        if d >= 2:
+            give_back(d - 2)
+
+    total = tot_f32[...]
+    for d in range(1, n_attn):
+        ret_copies[d].wait_recv()
+        total = total + ret_in[d - 1].astype(F32)
+    tot_f32[...] = total
+    tot[...] = total.astype(BF16)
+    fin_copies = [
+        send(
+            tot.at[lax.rem(x + dx, n_sect)],
+            fin_in.at[x],
+            fin_s.at[dx - 1],
+            fin_r.at[dx - 1],
+            sect=lax.rem(x + dx, n_sect),
+        )
+        for dx in range(1, n_sect)
+    ]
+    fin_f32[x] = tot_f32[x]
+    for dx in range(1, n_sect):
+        fin_copies[dx - 1].wait_recv()
+        from_x = lax.rem(x + (n_sect - dx), n_sect)
+        fin_f32[from_x] = fin_in[from_x].astype(F32)
+    joined = jnp.concatenate([fin_f32[i] for i in range(n_sect)], axis=1)
+    out_ref[...] = (mixed_f32 + joined).astype(BF16)
+    for copy in sends:
+        copy.wait_send()
+
+
+def on_device(
+    shape,
+    queries,
+    kv_pool,
+    block_list,
+    cache_len,
+    out_weight,
+    residual,
+    norm_gain,
+    router,
+    expert_ids,
+    w_gate,
+    w_up,
+    w_down,
+):
+    a, s, p = shape["attn"], shape["sect"], shape["pair"]
+    q = s * p
+    group_rows, head_cols = queries.shape
+    own, width = residual.shape
+    heads_rows, span = out_weight.shape
+    hidden_part = w_gate.shape[2]
+    hidden_all, out_cols = w_down.shape[1:]
+    key_rows, key_cols = kv_pool.shape[2:]
+    wide = width + LANES
+    buffers = [
+        ((heads_rows, span), BF16),
+        ((width, hidden_part), BF16),
+        ((width, hidden_part), BF16),
+        ((hidden_all, out_cols), BF16),
+        ((a * kv_pool.shape[1], key_rows, key_cols), BF16),
+        ((a, group_rows, head_cols), BF16),
+        ((a, q, own, span), F32),
+        ((a, q, own, span), BF16),
+        ((a, q - 1, own, span), BF16),
+        ((a - 1, own, span), BF16),
+        ((a, own, span), BF16),
+        ((a, own, span), F32),
+        ((width, LANES), BF16),
+        ((a, q, own, wide), BF16),
+        ((a, s, q * own, hidden_part), BF16),
+        ((a, p, s, own, out_cols), F32),
+        ((a, p, s, own, out_cols), BF16),
+        ((a, p - 1, s, own, out_cols), BF16),
+        ((a - 1, s, own, out_cols), BF16),
+        ((a - 1, s, own, out_cols), BF16),
+        ((s, own, out_cols), F32),
+        ((s, own, out_cols), BF16),
+        ((s, own, out_cols), BF16),
+        ((s, own, out_cols), F32),
+    ]
+    held = sum(math.prod(dims) * jnp.dtype(kind).itemsize for dims, kind in buffers)
+    fits = (
+        2 * held <= VMEM_BYTES
+        and span % LANES == 0
+        and out_cols % LANES == 0
+        and hidden_part % LANES == 0
+        and w_gate.shape[0] == 1
+        and router.shape[1] <= LANES
+        and min(a, s, p) > 1
+        and own % 16 == 0
+        and group_rows == q * own
+    )
+    if not fits:
+        return by_collectives(
+            queries,
+            kv_pool,
+            block_list,
+            cache_len,
+            out_weight,
+            residual,
+            norm_gain,
+            router,
+            expert_ids,
+            w_gate,
+            w_up,
+            w_down,
+        )
+    sems = [
+        (4,),
+        (a - 1,),
+        (a - 1,),
+        (a - 1,),
+        (a - 1,),
+        (a, q - 1),
+        (a, q - 1),
+        (a - 1,),
+        (a - 1,),
+        (a - 1,),
+        (a - 1,),
+        (a, s - 1),
+        (a, s - 1),
+        (a, s, p - 1),
+        (a, s, p - 1),
+        (a, s - 1),
+        (a, s - 1),
+        (a, p - 1),
+        (a, p - 1),
+        (a - 1,),
+        (a - 1,),
+        (s - 1,),
+        (s - 1,),
+    ]
+    vmem = pl.BlockSpec(memory_space=pltpu.VMEM)
+    smem = pl.BlockSpec(memory_space=pltpu.SMEM)
+    hbm = pl.BlockSpec(memory_space=pl.ANY)
+    return pl.pallas_call(
+        functools.partial(layer_kernel, (a, s, p)),
+        out_shape=jax.ShapeDtypeStruct(residual.shape, BF16),
+        in_specs=[vmem, vmem, smem, smem, vmem, vmem, vmem, vmem, hbm, hbm, hbm, hbm],
+        out_specs=vmem,
+        scratch_shapes=[pltpu.VMEM(dims, kind) for dims, kind in buffers]
+        + [pltpu.SemaphoreType.DMA(dims) for dims in sems],
+        compiler_params=pltpu.CompilerParams(
+            collective_id=0, has_side_effects=True, vmem_limit_bytes=VMEM_BYTES
+        ),
+    )(
+        queries,
+        kv_pool,
+        block_list,
+        cache_len,
+        residual,
+        norm_gain.reshape(1, -1),
+        router,
+        expert_ids,
+        out_weight,
+        w_gate,
+        w_up,
+        w_down,
+    )
+
+
 def solution(mesh):
     placed = (
         P(("group", "attn"), ("sect", "pair")),
@@ -122,7 +659,7 @@
         P(("attn", "pair"), None, "sect"),
     )
     return jax.shard_map(
-        on_device,
+        functools.partial(on_device, dict(mesh.shape)),
         mesh=mesh,
         in_specs=placed,
         out_specs=P(("group", "attn", "sect", "pair"), None),

time: 218 us -> 74.4 us (0.34)
  waiting for transfers between devices: 117 us -> 0 us
  Pallas kernels: 0 us -> 62.8 us
  blocking collectives: 57.4 us -> 0 us
  between operations: 14 us -> 0.68 us
  matrix products: 8.49 us -> 0 us
  starting transfers between devices: 4.68 us -> 0 us
  other arithmetic: 3.71 us -> 0 us
    all_gather x2 -> x0, waiting for transfers between devices: 83 us -> none  [the longest x1 63.6 us: on_device(): lax.all_gather(out_weight, 'attn', axis=1, tiled=True)]
    pallas_call x0 -> x1, Pallas kernels: none -> 62.8 us  [on_device(): pl.pallas_call(functools.partial(layer_kernel, (a, s, p)), out_shape=jax....]
    all_to_all x2 -> x0, blocking collectives: 29.7 us -> none  [the longest x1 19.9 us: on_device(): lax.all_to_all(outgoing, ('attn', 'pair'), split_axis=0, concat_axis=0, t...]
    all_gather x2 -> x0, blocking collectives: 27.7 us -> none  [the longest x1 20.4 us: on_device(): pool_all = lax.all_gather(kv_pool, 'attn', axis=1, tiled=True)]
    reduce_scatter x1 -> x0, waiting for transfers between devices: 19.7 us -> none  [on_device(): lax.psum_scatter(partial_value, ('sect', 'pair'), scatter_dimension=0, ti...]
    all_to_all x1 -> x0, waiting for transfers between devices: 13.7 us -> none  [on_device(): lax.all_to_all(segmented[0], ('attn', 'pair'), split_axis=0, concat_axis=...]
    unnamed x19, local copies, waits for them, and re-layouts: 0.12 us -> 10.5 us
    dot_general x6 -> x0, matrix products: 8.09 us -> none  [the longest x1 3.86 us: on_device(): jnp.dot(attended, lax.all_gather(out_weight, 'attn', axis=1, tiled=True),...]
  transfers between devices with their start and end apart: 4 -> 0, of which waited for: 4 -> 0; matrix products, arithmetic and copies ran while one was open for 2% -> 0% of each run, Pallas kernels for 0% -> 0%
where the time goes in v1:
time: 74.4 us; the launch traced here: 73.9 us
  Pallas kernels  62.8 us (84%)
  local copies, waits for them, and re-layouts  10.5 us (14%)
    pallas_call x1, Pallas kernels, on_device(): pl.pallas_call(functools.partial(layer_kernel, (a, s, p)), out_shape=jax....  62.8 us
    unnamed x19, local copies, waits for them, and re-layouts  10.5 us

profile of v1, /device:TPU:0, one launch (start us, length us, event | category | flops | bytes accessed | tf_op | source)
XLA Modules:
  0.0 73.9 jit_solution(2133010411740667244)
XLA Ops:
  0.7 0.8 %copy.14.ids_ref = s32[16,4]{1,0:T(8,128)S(1)} copy(s32[16,4]{0,1:T(4,128)} %param.20) | data formatting | bytes 512 | tf_op args[8]
  1.4 1.0 %copy.13.router_ref = bf16[2048,8]{1,0:T(8,128)(2,1)S(1)} copy(bf16[2048,8]{0,1:T(8,128)(2,1)} %param.19) | data formatting | bytes 65536 | tf_op args[7]
  2.4 0.0 copy-start
  2.5 1.4 %copy-done = bf16[1,2048,384]{2,1,0:T(8,128)(2,1)S(1)} copy-done((bf16[1,2048,384]{2,1,0:T(8,128)(2,1)S(1)}, bf16[1,2048,384]{2,1,0:T(8,128)(2,1)}, u32[]{:S(2)}) %copy-start) | copy-done | bytes 1572888
  3.9 0.0 copy-start.1
  3.9 1.4 %copy-done.1 = bf16[1,2048,384]{2,1,0:T(8,128)(2,1)S(1)} copy-done((bf16[1,2048,384]{2,1,0:T(8,128)(2,1)S(1)}, bf16[1,2048,384]{2,1,0:T(8,128)(2,1)}, u32[]{:S(2)}) %copy-start.1) | copy-done | bytes 1572888
  5.3 0.0 copy-start.2
  5.3 1.2 %copy-done.2 = bf16[1024,512]{1,0:T(8,128)(2,1)S(1)} copy-done((bf16[1024,512]{1,0:T(8,128)(2,1)S(1)}, bf16[1024,512]{1,0:T(8,128)(2,1)}, u32[]{:S(2)}) %copy-start.2) | copy-done | bytes 1048600
  6.5 0.0 copy-start.3
  6.5 0.9 %copy-done.3 = bf16[64,1024]{1,0:T(8,128)(2,1)S(1)} copy-done((bf16[64,1024]{1,0:T(8,128)(2,1)S(1)}, bf16[64,1024]{1,0:T(8,128)(2,1)}, u32[]{:S(2)}) %copy-start.3) | copy-done | bytes 131096
  7.4 0.0 copy-start.4
  7.4 0.9 %copy-done.4 = bf16[2,1,128,256]{3,2,1,0:T(8,128)(2,1)S(1)} copy-done((bf16[2,1,128,256]{3,2,1,0:T(8,128)(2,1)S(1)}, bf16[2,1,128,256]{3,2,1,0:T(8,128)(2,1)}, u32[]{:S(2)}) %copy-start.4) | copy-done | bytes 131096
  8.3 0.0 copy-start.5
  8.3 0.8 %copy-done.5 = bf16[16,2048]{1,0:T(8,128)(2,1)S(1)} copy-done((bf16[16,2048]{1,0:T(8,128)(2,1)S(1)}, bf16[16,2048]{1,0:T(8,128)(2,1)}, u32[]{:S(2)}) %copy-start.5) | copy-done | bytes 65560
  9.1 0.0 copy-start.6
  9.1 0.7 copy-done.6
  9.8 0.0 copy-start.7
  9.8 0.7 copy-done.7
  10.5 62.8 %shard_map.118 = bf16[16,2048]{1,0:T(8,128)(2,1)S(1)} custom-call(bf16[64,1024]{1,0:T(8,128)(2,1)S(1)} %copy-done.3, bf16[2,1,128,256]{3,2,1,0:T(8,128)(2,1)S(1)} %copy-done.4, s32[1,2]{1,0:T(1,128)S(1)} %copy-done.7, s32[1]{0:T(128)S(6)} %copy.16.len_ref, bf16[16,2048]{1,0:T(8,128)(2,1)S(1)} %copy-done.5, f32[1,2048]{1,0:T(1,128)S(1)} %bitcast.1, ...), custom_call_target="tpu_custom_call" | custom-call | tf_op jit(solution)/shard_map/pallas_call | solution.py:620
  73.3 0.6 copy.17
Async XLA Ops:
  2.4 1.4 %copy-start = (bf16[1,2048,384]{2,1,0:T(8,128)(2,1)S(1)}, bf16[1,2048,384]{2,1,0:T(8,128)(2,1)}, u32[]{:S(2)}) copy-start(bf16[1,2048,384]{2,1,0:T(8,128)(2,1)} %wg_hbm.1) | copy-start | bytes 4718596
  3.9 1.4 %copy-start.1 = (bf16[1,2048,384]{2,1,0:T(8,128)(2,1)S(1)}, bf16[1,2048,384]{2,1,0:T(8,128)(2,1)}, u32[]{:S(2)}) copy-start(bf16[1,2048,384]{2,1,0:T(8,128)(2,1)} %wu_hbm.1) | copy-start | bytes 4718596
  5.3 1.2 %copy-start.2 = (bf16[1024,512]{1,0:T(8,128)(2,1)S(1)}, bf16[1024,512]{1,0:T(8,128)(2,1)}, u32[]{:S(2)}) copy-start(bf16[1024,512]{1,0:T(8,128)(2,1)} %wo_hbm.1) | copy-start | bytes 3145732
  6.5 0.9 %copy-start.3 = (bf16[64,1024]{1,0:T(8,128)(2,1)S(1)}, bf16[64,1024]{1,0:T(8,128)(2,1)}, u32[]{:S(2)}) copy-start(bf16[64,1024]{1,0:T(8,128)(2,1)} %q_ref.1) | copy-start | bytes 393220
  7.4 0.9 %copy-start.4 = (bf16[2,1,128,256]{3,2,1,0:T(8,128)(2,1)S(1)}, bf16[2,1,128,256]{3,2,1,0:T(8,128)(2,1)}, u32[]{:S(2)}) copy-start(bf16[2,1,128,256]{3,2,1,0:T(8,128)(2,1)} %kv_ref.1) | copy-start | bytes 393220
  8.3 0.8 %copy-start.5 = (bf16[16,2048]{1,0:T(8,128)(2,1)S(1)}, bf16[16,2048]{1,0:T(8,128)(2,1)}, u32[]{:S(2)}) copy-start(bf16[16,2048]{1,0:T(8,128)(2,1)} %res_ref.1) | copy-start | bytes 196612
  9.1 0.7 copy-start.6
  9.8 0.7 copy-start.7

commit v2 on v1

--- a/solution.py
+++ b/solution.py
@@ -111,26 +111,31 @@
 
 MESH = pl.DeviceIdType.MESH
 LANES = 128
-VMEM_BYTES = 48 * 1024 * 1024
+VMEM_BYTES = 60 * 1024 * 1024
 BF16 = jnp.bfloat16
 F32 = jnp.float32
 
 
 def layer_kernel(
     sizes,
-    q_ref,
-    kv_ref,
-    list_ref,
-    len_ref,
-    res_ref,
-    gain_ref,
-    router_ref,
-    ids_ref,
+    q_hbm,
+    kv_hbm,
+    list_hbm,
+    len_hbm,
+    res_hbm,
+    gain_hbm,
+    router_hbm,
+    ids_hbm,
     wo_hbm,
     wg_hbm,
     wu_hbm,
     wd_hbm,
     out_ref,
+    q_ref,
+    res_ref,
+    gain_ref,
+    router_ref,
+    ids_ref,
     wo,
     wg,
     wu,
@@ -143,7 +148,6 @@
     sum_out,
     mix_in,
     mix_f32,
-    router_pad,
     rows,
     hid,
     prod_f32,
@@ -155,6 +159,8 @@
     tot,
     fin_in,
     fin_f32,
+    list_ref,
+    len_ref,
     w_sem,
     kv_s,
     kv_r,
@@ -190,7 +196,8 @@
     group_rows, head_cols = q_ref.shape
     local_heads = head_cols // HEAD_DIM
     kv_local = c * local_heads // (HEADS // KV_HEADS)
-    blocks = kv_ref.shape[1]
+    blocks = kv_hbm.shape[1]
+    kv_slot = pl.ds(z * blocks, blocks)
     sends = []
 
     def send(src, dst, s_sem, r_sem, **where):
@@ -209,7 +216,20 @@
     loads = [
         pltpu.make_async_copy(src, dst, w_sem.at[i])
         for i, (src, dst) in enumerate(
-            ((wo_hbm, wo), (wg_hbm.at[0], wg), (wu_hbm.at[0], wu), (wd_hbm.at[0], wd))
+            (
+                (q_hbm, q_ref),
+                (kv_hbm.at[kv_local], kvbuf.at[kv_slot]),
+                (list_hbm, list_ref),
+                (len_hbm, len_ref),
+                (wo_hbm, wo),
+                (res_hbm, res_ref),
+                (gain_hbm, gain_ref),
+                (router_hbm, router_ref),
+                (ids_hbm, ids_ref),
+                (wg_hbm.at[0], wg),
+                (wu_hbm.at[0], wu),
+                (wd_hbm.at[0], wd),
+            )
         )
     ]
     for load in loads:
@@ -238,10 +258,9 @@
     def behind(d):
         return lax.rem(z + (n_attn - d), n_attn)
 
-    kv_slot = pl.ds(z * blocks, blocks)
     kv_copies = [
         send(
-            kv_ref.at[kv_local],
+            kv_hbm.at[kv_local],
             kvbuf.at[kv_slot],
             kv_s.at[d - 1],
             kv_r.at[d - 1],
@@ -249,9 +268,8 @@
         )
         for d in range(1, n_attn)
     ]
-    kvbuf[kv_slot] = kv_ref[kv_local]
-    router_pad[...] = jnp.zeros_like(router_pad)
-    router_pad[:, : router_ref.shape[1]] = router_ref[...]
+    for load in loads[:4]:
+        load.wait()
     for copy in kv_copies:
         copy.wait_recv()
 
@@ -267,7 +285,7 @@
         heads, keys, (((1,), (1,)), ((), ())), preferred_element_type=F32
     ) / math.sqrt(HEAD_DIM)
     place = lax.broadcasted_iota(jnp.int32, scores.shape, 1)
-    scores = jnp.where(place < len_ref[0], scores, -jnp.inf)
+    scores = jnp.where(place < len_ref[0, 0], scores, -jnp.inf)
     lifted = jnp.exp(scores - jnp.max(scores, axis=-1, keepdims=True))
     row_total = jnp.sum(lifted, axis=-1, keepdims=True)
     mixed = jnp.dot(lifted.astype(BF16), values, preferred_element_type=F32) / row_total
@@ -283,7 +301,7 @@
     def plane(step):
         return lax.div(step, n_pair), lax.rem(step, n_pair)
 
-    loads[0].wait()
+    loads[4].wait()
     rs_copies = []
     mix_copies = []
 
@@ -339,6 +357,9 @@
         mix_copies[d - 1].wait_recv()
         mix_f32[ahead(d)] = mix_in[ahead(d)].astype(F32)
 
+    for load in loads[5:9]:
+        load.wait()
+
     span = width // n_attn
     mixed_f32 = res_ref[...].astype(F32) + jnp.concatenate(
         [mix_f32[a] for a in range(n_attn)], axis=1
@@ -349,14 +370,22 @@
         * lax.rsqrt(jnp.mean(mixed_f32 * mixed_f32, axis=-1, keepdims=True) + 1e-06)
         * gain_ref[...]
     ).astype(BF16)
-    logits = jnp.dot(normed, router_pad[...], preferred_element_type=F32)
-    lane = lax.broadcasted_iota(jnp.int32, logits.shape, 1)
-    chosen = lane == ids_ref[:, 0:1]
-    for k in range(1, ids_ref.shape[1]):
-        chosen = jnp.logical_or(chosen, lane == ids_ref[:, k : k + 1])
+    logits = lax.dot_general(
+        router_ref[...], normed, (((1,), (1,)), ((), ())), preferred_element_type=F32
+    )
+    lane = lax.broadcasted_iota(jnp.int32, logits.shape, 0)
+    chosen = lane == ids_ref[0:1, :]
+    for k in range(1, ids_ref.shape[0]):
+        chosen = jnp.logical_or(chosen, lane == ids_ref[k : k + 1, :])
     logits = jnp.where(chosen, logits, -jnp.inf)
-    raised = jnp.exp(logits - jnp.max(logits, axis=-1, keepdims=True))
-    route = raised / jnp.sum(raised, axis=-1, keepdims=True)
+    raised = jnp.exp(logits - jnp.max(logits, axis=0, keepdims=True))
+    route = raised / jnp.sum(raised, axis=0, keepdims=True)
+    route = jnp.concatenate(
+        [route, jnp.zeros((LANES - route.shape[0], own), F32)], axis=0
+    )
+    route = jnp.transpose(
+        jnp.concatenate([route, jnp.zeros((LANES, LANES - own), F32)], axis=1)
+    )[:own]
     rows[0, quarter, :, :width] = normed
     rows[0, quarter, :, width:] = route.astype(BF16)
 
@@ -372,7 +401,7 @@
     ]
     nx_copies = [None] * n_attn
     nc_copies = [None] * n_attn
-    for load in loads[1:]:
+    for load in loads[9:]:
         load.wait()
 
     def to_cores(d, dx):
@@ -474,16 +503,24 @@
             )
 
     spread(0)
-    for d in range(n_attn + 2):
-        if d + 1 < n_attn:
-            spread(d + 1)
-        if d < n_attn:
-            spread_on(d)
-            up(d)
-        if 1 <= d <= n_attn:
-            down(d - 1)
-        if d >= 2:
-            give_back(d - 2)
+    spread_on(0)
+    up(0)
+    for d in range(1, n_attn):
+        spread(d)
+        if d == 1:
+            down(0)
+        else:
+            spread_on(d - 1)
+            up(d - 1)
+        if d == 2:
+            give_back(0)
+    spread_on(n_attn - 1)
+    up(n_attn - 1)
+    for d in range(1, n_attn):
+        down(d)
+        if d > 1:
+            give_back(d - 1)
+    give_back(n_attn - 1)
 
     total = tot_f32[...]
     for d in range(1, n_attn):
@@ -537,6 +574,11 @@
     key_rows, key_cols = kv_pool.shape[2:]
     wide = width + LANES
     buffers = [
+        ((group_rows, head_cols), BF16),
+        ((own, width), BF16),
+        ((1, width), F32),
+        (router.shape[::-1], BF16),
+        (expert_ids.shape[::-1], jnp.int32),
         ((heads_rows, span), BF16),
         ((width, hidden_part), BF16),
         ((width, hidden_part), BF16),
@@ -549,7 +591,6 @@
         ((a - 1, own, span), BF16),
         ((a, own, span), BF16),
         ((a, own, span), F32),
-        ((width, LANES), BF16),
         ((a, q, own, wide), BF16),
         ((a, s, q * own, hidden_part), BF16),
         ((a, p, s, own, out_cols), F32),
@@ -572,6 +613,7 @@
         and router.shape[1] <= LANES
         and min(a, s, p) > 1
         and own % 16 == 0
+        and own <= LANES
         and group_rows == q * own
     )
     if not fits:
@@ -590,7 +632,7 @@
             w_down,
         )
     sems = [
-        (4,),
+        (12,),
         (a - 1,),
         (a - 1,),
         (a - 1,),
@@ -615,14 +657,14 @@
         (s - 1,),
     ]
     vmem = pl.BlockSpec(memory_space=pltpu.VMEM)
-    smem = pl.BlockSpec(memory_space=pltpu.SMEM)
-    hbm = pl.BlockSpec(memory_space=pl.ANY)
+    hbm = pl.BlockSpec(memory_space=pltpu.HBM)
     return pl.pallas_call(
         functools.partial(layer_kernel, (a, s, p)),
         out_shape=jax.ShapeDtypeStruct(residual.shape, BF16),
-        in_specs=[vmem, vmem, smem, smem, vmem, vmem, vmem, vmem, hbm, hbm, hbm, hbm],
+        in_specs=[hbm] * 12,
         out_specs=vmem,
         scratch_shapes=[pltpu.VMEM(dims, kind) for dims, kind in buffers]
+        + [pltpu.SMEM(block_list.shape, jnp.int32), pltpu.SMEM((1, 1), jnp.int32)]
         + [pltpu.SemaphoreType.DMA(dims) for dims in sems],
         compiler_params=pltpu.CompilerParams(
             collective_id=0, has_side_effects=True, vmem_limit_bytes=VMEM_BYTES
@@ -631,11 +673,11 @@
         queries,
         kv_pool,
         block_list,
-        cache_len,
+        cache_len.reshape(1, -1),
         residual,
         norm_gain.reshape(1, -1),
-        router,
-        expert_ids,
+        router.T,
+        expert_ids.T,
         out_weight,
         w_gate,
         w_up,

time: 74.4 us -> 65.8 us (0.88)
  local copies, waits for them, and re-layouts: 10.5 us -> 1.47 us
    unnamed x19 -> x1, local copies, waits for them, and re-layouts: 10.5 us -> 1.47 us
where the time goes in v2:
time: 65.8 us; the launch traced here: 65.6 us
  Pallas kernels  63.5 us (97%)
  local copies, waits for them, and re-layouts  1.47 us (2%)
  between operations  0.66 us (1%)
    pallas_call x1, Pallas kernels, on_device(): pl.pallas_call(functools.partial(layer_kernel, (a, s, p)), out_shape=jax....  63.5 us
    unnamed x1, local copies, waits for them, and re-layouts  1.47 us

profile of v2, /device:TPU:0, one launch (start us, length us, event | category | flops | bytes accessed | tf_op | source)
XLA Modules:
  0.0 65.6 jit_solution(1178025596957043942)
XLA Ops:
  0.7 63.5 %shard_map.118 = bf16[16,2048]{1,0:T(8,128)(2,1)} custom-call(bf16[64,1024]{1,0:T(8,128)(2,1)} %q_hbm.1, bf16[2,1,128,256]{3,2,1,0:T(8,128)(2,1)} %kv_hbm.1, s32[1,2]{1,0:T(1,128)} %list_hbm.1, s32[1,1]{1,0:T(1,128)} %bitcast.4.len_hbm, bf16[16,2048]{1,0:T(8,128)(2,1)} %res_hbm.1, f32[1,2048]{1,0:T(1,128)} %bitcast.6, bf16[8,2048]{1,0:T(8,128)(2,1)} %bitcast.5, ...), custom_call_target="tpu_custom_call" | custom-call | tf_op jit(solution)/shard_map/pallas_call | solution.py:661
  64.1 1.5 %copy.15 = bf16[16,2048]{1,0:T(8,128)(2,1)} copy(bf16[16,2048]{1,0:T(8,128)(2,1)} %shard_map.118) | data formatting | bytes 131072

commit v3 on v2

--- a/solution.py
+++ b/solution.py
@@ -149,16 +149,14 @@
     mix_in,
     mix_f32,
     rows,
-    hid,
     prod_f32,
     prod,
     pair_in,
+    sect_f32,
+    sect,
+    sect_in,
     ret_out,
     ret_in,
-    tot_f32,
-    tot,
-    fin_in,
-    fin_f32,
     list_ref,
     len_ref,
     w_sem,
@@ -176,14 +174,14 @@
     nx_r,
     nc_s,
     nc_r,
-    hid_s,
-    hid_r,
+    wd_s,
+    wd_r,
     pair_s,
     pair_r,
+    sect_s,
+    sect_r,
     ret_s,
     ret_r,
-    fin_s,
-    fin_r,
 ):
     n_attn, n_sect, n_pair = sizes
     quarters = n_sect * n_pair
@@ -198,6 +196,7 @@
     kv_local = c * local_heads // (HEADS // KV_HEADS)
     blocks = kv_hbm.shape[1]
     kv_slot = pl.ds(z * blocks, blocks)
+    hidden_part = wg.shape[1]
     sends = []
 
     def send(src, dst, s_sem, r_sem, **where):
@@ -228,7 +227,7 @@
                 (ids_hbm, ids_ref),
                 (wg_hbm.at[0], wg),
                 (wu_hbm.at[0], wu),
-                (wd_hbm.at[0], wd),
+                (wd_hbm.at[0, pl.ds(x * hidden_part, hidden_part)], wd.at[x]),
             )
         )
     ]
@@ -268,6 +267,18 @@
         )
         for d in range(1, n_attn)
     ]
+    wd_copies = []
+    for dx in range(1, n_sect):
+        to_x = lax.rem(x + dx, n_sect)
+        wd_copies.append(
+            send(
+                wd_hbm.at[0, pl.ds(to_x * hidden_part, hidden_part)],
+                wd.at[x],
+                wd_s.at[dx - 1],
+                wd_r.at[dx - 1],
+                sect=to_x,
+            )
+        )
     for load in loads[:4]:
         load.wait()
     for copy in kv_copies:
@@ -403,6 +414,8 @@
     nc_copies = [None] * n_attn
     for load in loads[9:]:
         load.wait()
+    for copy in wd_copies:
+        copy.wait_recv()
 
     def to_cores(d, dx):
         from_q = lax.rem(x + (n_sect - dx), n_sect) * n_pair + c
@@ -437,7 +450,7 @@
             nx_copies[d][dx - 1].wait_recv()
             nc_copies[d] += to_cores(d, dx)
 
-    hid_copies = [None] * n_attn
+    sect_copies = [None] * n_attn
     pair_copies = [None] * n_attn
     ret_copies = [None] * n_attn
     expert = z * n_pair + c
@@ -448,23 +461,11 @@
         tokens = rows[d].reshape(quarters * own, rows.shape[-1])[:, :width]
         gate_val = jnp.dot(tokens, wg[...], preferred_element_type=F32)
         up_val = jnp.dot(tokens, wu[...], preferred_element_type=F32)
-        hid[d, x] = (gate_val / (1.0 + jnp.exp(-gate_val)) * up_val).astype(BF16)
-        hid_copies[d] = [
-            send(
-                hid.at[d, x],
-                hid.at[d, x],
-                hid_s.at[d, dx - 1],
-                hid_r.at[d, dx - 1],
-                sect=lax.rem(x + dx, n_sect),
-            )
-            for dx in range(1, n_sect)
-        ]
-
-    def down(d):
-        for copy in hid_copies[d]:
-            copy.wait_recv()
-        hidden = jnp.concatenate([hid[d, i] for i in range(n_sect)], axis=1)
-        value = jnp.dot(hidden, wd[...], preferred_element_type=F32)
+        hidden = (gate_val / (1.0 + jnp.exp(-gate_val)) * up_val).astype(BF16)
+        value = jnp.concatenate(
+            [jnp.dot(hidden, wd[i], preferred_element_type=F32) for i in range(n_sect)],
+            axis=1,
+        )
         weights = rows[d].reshape(quarters * own, rows.shape[-1])[:, width:].astype(F32)
         lanes = lax.broadcasted_iota(jnp.int32, weights.shape, 1)
         weight = jnp.sum(jnp.where(lanes == expert, weights, 0.0), axis=-1, keepdims=True)
@@ -484,66 +485,66 @@
             for dc in range(1, n_pair)
         ]
 
-    def give_back(d):
+    def to_sect(d):
         for copy in pair_copies[d]:
             copy.wait_recv()
         total = prod_f32[d, c]
         for j in range(n_pair - 1):
             total = total + pair_in[d, j].astype(F32)
+        sect_f32[d] = total
+        sect[d] = total.astype(BF16)
+        sect_copies[d] = [
+            send(
+                sect.at[d, lax.rem(x + dx, n_sect)],
+                sect_in.at[d, dx - 1],
+                sect_s.at[d, dx - 1],
+                sect_r.at[d, dx - 1],
+                sect=lax.rem(x + dx, n_sect),
+            )
+            for dx in range(1, n_sect)
+        ]
+
+    def give_back(d):
+        for copy in sect_copies[d]:
+            copy.wait_recv()
+        total = sect_f32[d, x]
+        for j in range(n_sect - 1):
+            total = total + sect_in[d, j].astype(F32)
         if d == 0:
-            tot_f32[...] = total
-        else:
-            ret_out[d - 1] = total.astype(BF16)
-            ret_copies[d] = send(
-                ret_out.at[d - 1],
-                ret_in.at[d - 1],
-                ret_s.at[d - 1],
-                ret_r.at[d - 1],
-                attn=behind(d),
-            )
+            return total
+        ret_out[d - 1] = total.astype(BF16)
+        ret_copies[d] = send(
+            ret_out.at[d - 1],
+            ret_in.at[d - 1],
+            ret_s.at[d - 1],
+            ret_r.at[d - 1],
+            attn=behind(d),
+        )
 
     spread(0)
     spread_on(0)
     up(0)
+    turns = list(range(1, n_attn)) + [0]
+    early = max(0, n_attn - 3)
     for d in range(1, n_attn):
         spread(d)
-        if d == 1:
-            down(0)
-        else:
+        if d >= 2:
             spread_on(d - 1)
             up(d - 1)
-        if d == 2:
-            give_back(0)
+        if d >= 3:
+            to_sect(d - 2)
     spread_on(n_attn - 1)
     up(n_attn - 1)
-    for d in range(1, n_attn):
-        down(d)
-        if d > 1:
-            give_back(d - 1)
-    give_back(n_attn - 1)
-
-    total = tot_f32[...]
+    for i in range(early - 1):
+        give_back(turns[i])
+    for i in range(early, n_attn):
+        to_sect(turns[i])
+        if i:
+            give_back(turns[i - 1])
+    joined = give_back(0)
     for d in range(1, n_attn):
         ret_copies[d].wait_recv()
-        total = total + ret_in[d - 1].astype(F32)
-    tot_f32[...] = total
-    tot[...] = total.astype(BF16)
-    fin_copies = [
-        send(
-            tot.at[lax.rem(x + dx, n_sect)],
-            fin_in.at[x],
-            fin_s.at[dx - 1],
-            fin_r.at[dx - 1],
-            sect=lax.rem(x + dx, n_sect),
-        )
-        for dx in range(1, n_sect)
-    ]
-    fin_f32[x] = tot_f32[x]
-    for dx in range(1, n_sect):
-        fin_copies[dx - 1].wait_recv()
-        from_x = lax.rem(x + (n_sect - dx), n_sect)
-        fin_f32[from_x] = fin_in[from_x].astype(F32)
-    joined = jnp.concatenate([fin_f32[i] for i in range(n_sect)], axis=1)
+        joined = joined + ret_in[d - 1].astype(F32)
     out_ref[...] = (mixed_f32 + joined).astype(BF16)
     for copy in sends:
         copy.wait_send()
@@ -570,7 +571,7 @@
     own, width = residual.shape
     heads_rows, span = out_weight.shape
     hidden_part = w_gate.shape[2]
-    hidden_all, out_cols = w_down.shape[1:]
+    out_cols = w_down.shape[2]
     key_rows, key_cols = kv_pool.shape[2:]
     wide = width + LANES
     buffers = [
@@ -582,7 +583,7 @@
         ((heads_rows, span), BF16),
         ((width, hidden_part), BF16),
         ((width, hidden_part), BF16),
-        ((hidden_all, out_cols), BF16),
+        ((s, hidden_part, out_cols), BF16),
         ((a * kv_pool.shape[1], key_rows, key_cols), BF16),
         ((a, group_rows, head_cols), BF16),
         ((a, q, own, span), F32),
@@ -592,16 +593,14 @@
         ((a, own, span), BF16),
         ((a, own, span), F32),
         ((a, q, own, wide), BF16),
-        ((a, s, q * own, hidden_part), BF16),
-        ((a, p, s, own, out_cols), F32),
-        ((a, p, s, own, out_cols), BF16),
-        ((a, p - 1, s, own, out_cols), BF16),
-        ((a - 1, s, own, out_cols), BF16),
-        ((a - 1, s, own, out_cols), BF16),
-        ((s, own, out_cols), F32),
-        ((s, own, out_cols), BF16),
-        ((s, own, out_cols), BF16),
-        ((s, own, out_cols), F32),
+        ((a, p, s, own, width), F32),
+        ((a, p, s, own, width), BF16),
+        ((a, p - 1, s, own, width), BF16),
+        ((a, s, own, width), F32),
+        ((a, s, own, width), BF16),
+        ((a, s - 1, own, width), BF16),
+        ((a - 1, own, width), BF16),
+        ((a - 1, own, width), BF16),
     ]
     held = sum(math.prod(dims) * jnp.dtype(kind).itemsize for dims, kind in buffers)
     fits = (
@@ -615,6 +614,8 @@
         and own % 16 == 0
         and own <= LANES
         and group_rows == q * own
+        and hidden_part % 16 == 0
+        and out_cols * s == width
     )
     if not fits:
         return by_collectives(
@@ -647,14 +648,14 @@
         (a, s - 1),
         (a, s, p - 1),
         (a, s, p - 1),
+        (s - 1,),
+        (s - 1,),
+        (a, p - 1),
+        (a, p - 1),
         (a, s - 1),
         (a, s - 1),
-        (a, p - 1),
-        (a, p - 1),
-        (a - 1,),
-        (a - 1,),
-        (s - 1,),
-        (s - 1,),
+        (a - 1,),
+        (a - 1,),
     ]
     vmem = pl.BlockSpec(memory_space=pltpu.VMEM)
     hbm = pl.BlockSpec(memory_space=pltpu.HBM)

time: 65.8 us -> 62.7 us (0.953)
  Pallas kernels: 63.5 us -> 60.4 us
    pallas_call x1, Pallas kernels: 63.5 us -> 60.4 us  [on_device(): pl.pallas_call(functools.partial(layer_kernel, (a, s, p)), out_shape=jax....]
where the time goes in v3:
time: 62.7 us; the launch traced here: 62.5 us
  Pallas kernels  60.4 us (96%)
  local copies, waits for them, and re-layouts  1.47 us (2%)
  between operations  0.66 us (1%)
    pallas_call x1, Pallas kernels, on_device(): pl.pallas_call(functools.partial(layer_kernel, (a, s, p)), out_shape=jax....  60.4 us
    unnamed x1, local copies, waits for them, and re-layouts  1.47 us

profile of v3, /device:TPU:0, one launch (start us, length us, event | category | flops | bytes accessed | tf_op | source)
XLA Modules:
  0.0 62.5 jit_solution(9587490604177215502)
XLA Ops:
  0.7 60.4 %shard_map.118 = bf16[16,2048]{1,0:T(8,128)(2,1)} custom-call(bf16[64,1024]{1,0:T(8,128)(2,1)} %q_hbm.1, bf16[2,1,128,256]{3,2,1,0:T(8,128)(2,1)} %kv_hbm.1, s32[1,2]{1,0:T(1,128)} %list_hbm.1, s32[1,1]{1,0:T(1,128)} %bitcast.4.len_hbm, bf16[16,2048]{1,0:T(8,128)(2,1)} %res_hbm.1, f32[1,2048]{1,0:T(1,128)} %bitcast.6, bf16[8,2048]{1,0:T(8,128)(2,1)} %bitcast.5, ...), custom_call_target="tpu_custom_call" | custom-call | tf_op jit(solution)/shard_map/pallas_call | solution.py:662
  61.0 1.5 %copy.15 = bf16[16,2048]{1,0:T(8,128)(2,1)} copy(bf16[16,2048]{1,0:T(8,128)(2,1)} %shard_map.118) | data formatting | bytes 131072

commit v4 on v3

--- a/solution.py
+++ b/solution.py
@@ -289,25 +289,77 @@
     cache = jnp.concatenate(picked, axis=0)
     keys = cache[:, :HEAD_DIM]
     values = cache[:, HEAD_DIM:]
-    heads = jnp.concatenate(
-        [q_ref[:, h * HEAD_DIM : (h + 1) * HEAD_DIM] for h in range(local_heads)], axis=0
-    )
-    scores = lax.dot_general(
-        heads, keys, (((1,), (1,)), ((), ())), preferred_element_type=F32
-    ) / math.sqrt(HEAD_DIM)
-    place = lax.broadcasted_iota(jnp.int32, scores.shape, 1)
-    scores = jnp.where(place < len_ref[0, 0], scores, -jnp.inf)
-    lifted = jnp.exp(scores - jnp.max(scores, axis=-1, keepdims=True))
-    row_total = jnp.sum(lifted, axis=-1, keepdims=True)
-    mixed = jnp.dot(lifted.astype(BF16), values, preferred_element_type=F32) / row_total
-    for h in range(local_heads):
-        att[0, :, h * HEAD_DIM : (h + 1) * HEAD_DIM] = mixed[
-            h * group_rows : (h + 1) * group_rows
-        ].astype(BF16)
-    att_copies = [None] + [
-        send(att.at[0], att.at[d], att_s.at[d - 1], att_r.at[d - 1], attn=ahead(d))
-        for d in range(1, n_attn)
-    ]
+    pieces, piece_cols = att.shape[1], att.shape[3]
+    last = n_attn - 1
+
+    def hop(src, piece, to, sem):
+        return pltpu.make_async_remote_copy(
+            src_ref=att.at[src, piece],
+            dst_ref=att.at[src, piece],
+            send_sem=sem,
+            recv_sem=att_r.at[src, piece],
+            device_id={"attn": to},
+            device_id_type=MESH,
+        )
+
+    piece_heads = piece_cols // HEAD_DIM
+    for piece in range(pieces):
+        start = piece * piece_cols
+        heads = jnp.concatenate(
+            [
+                q_ref[:, start + h * HEAD_DIM : start + (h + 1) * HEAD_DIM]
+                for h in range(piece_heads)
+            ],
+            axis=0,
+        )
+        scores = lax.dot_general(
+            heads, keys, (((1,), (1,)), ((), ())), preferred_element_type=F32
+        ) / math.sqrt(HEAD_DIM)
+        place = lax.broadcasted_iota(jnp.int32, scores.shape, 1)
+        scores = jnp.where(place < len_ref[0, 0], scores, -jnp.inf)
+        lifted = jnp.exp(scores - jnp.max(scores, axis=-1, keepdims=True))
+        row_total = jnp.sum(lifted, axis=-1, keepdims=True)
+        mixed = jnp.dot(lifted.astype(BF16), values, preferred_element_type=F32) / row_total
+        for h in range(piece_heads):
+            att[z, piece, :, h * HEAD_DIM : (h + 1) * HEAD_DIM] = mixed[
+                h * group_rows : (h + 1) * group_rows
+            ].astype(BF16)
+
+        @pl.when(z < last)
+        def _(piece=piece):
+            hop(z, piece, z + 1, att_s.at[0, piece, 1]).start()
+
+        @pl.when(z > 0)
+        def _(piece=piece):
+            hop(z, piece, z - 1, att_s.at[0, piece, 0]).start()
+
+    longer = jnp.where(2 * z > last, -1, 1)
+    shorter = jnp.minimum(z, last - z)
+
+    def nearest(i):
+        if i == 0:
+            return z
+        j = i - 1
+        paired = j < 2 * shorter
+        reach = jnp.where(paired, j // 2 + 1, j - shorter + 1)
+        if j % 2:
+            return z + jnp.where(paired, -longer, longer) * reach
+        return z + longer * reach
+
+    def goes_on(src):
+        return jnp.where(src < z, last - z, z) > 0
+
+    def onward(src):
+        return jnp.where(src < z, z + 1, z - 1)
+
+    def arrive(i):
+        src = nearest(i)
+        for piece in range(pieces):
+            hop(src, piece, ahead(1), att_s.at[i, piece, 0]).wait_recv()
+
+            @pl.when(goes_on(src))
+            def _(piece=piece):
+                hop(src, piece, onward(src), att_s.at[i, piece, 0]).start()
 
     def plane(step):
         return lax.div(step, n_pair), lax.rem(step, n_pair)
@@ -318,8 +370,15 @@
 
     def project(d):
         if d:
-            att_copies[d].wait_recv()
-        value = jnp.dot(att[d], wo[...], preferred_element_type=F32)
+            arrive(d)
+        src = nearest(d)
+        value = jnp.dot(att[src, 0], wo[:piece_cols], preferred_element_type=F32)
+        for piece in range(1, pieces):
+            value += jnp.dot(
+                att[src, piece],
+                wo[piece * piece_cols : (piece + 1) * piece_cols],
+                preferred_element_type=F32,
+            )
         value = value.reshape(part_f32.shape[1:])
         part_f32[d] = value
         part[d] = value.astype(BF16)
@@ -354,8 +413,8 @@
                     sum_out.at[d - 1],
                     mix_in.at[z],
                     mix_s.at[d - 1],
-                    mix_r.at[d - 1],
-                    attn=behind(d),
+                    mix_r.at[z],
+                    attn=nearest(d),
                 )
             )
 
@@ -365,7 +424,14 @@
         if d:
             pass_on(d - 1)
     for d in range(1, n_attn):
-        mix_copies[d - 1].wait_recv()
+        pltpu.make_async_remote_copy(
+            src_ref=sum_out.at[d - 1],
+            dst_ref=mix_in.at[ahead(d)],
+            send_sem=mix_s.at[d - 1],
+            recv_sem=mix_r.at[ahead(d)],
+            device_id={"attn": ahead(d)},
+            device_id_type=MESH,
+        ).wait_recv()
         mix_f32[ahead(d)] = mix_in[ahead(d)].astype(F32)
 
     for load in loads[5:9]:
@@ -548,6 +614,22 @@
     out_ref[...] = (mixed_f32 + joined).astype(BF16)
     for copy in sends:
         copy.wait_send()
+    for piece in range(pieces):
+
+        @pl.when(z < last)
+        def _(piece=piece):
+            hop(z, piece, z + 1, att_s.at[0, piece, 1]).wait_send()
+
+        @pl.when(z > 0)
+        def _(piece=piece):
+            hop(z, piece, z - 1, att_s.at[0, piece, 0]).wait_send()
+
+        for i in range(1, n_attn):
+            src = nearest(i)
+
+            @pl.when(goes_on(src))
+            def _(piece=piece, i=i, src=src):
+                hop(src, piece, onward(src), att_s.at[i, piece, 0]).wait_send()
 
 
 def on_device(
@@ -574,6 +656,7 @@
     out_cols = w_down.shape[2]
     key_rows, key_cols = kv_pool.shape[2:]
     wide = width + LANES
+    pieces = 2 - head_cols // HEAD_DIM % 2
     buffers = [
         ((group_rows, head_cols), BF16),
         ((own, width), BF16),
@@ -585,7 +668,7 @@
         ((width, hidden_part), BF16),
         ((s, hidden_part, out_cols), BF16),
         ((a * kv_pool.shape[1], key_rows, key_cols), BF16),
-        ((a, group_rows, head_cols), BF16),
+        ((a, pieces, group_rows, head_cols // pieces), BF16),
         ((a, q, own, span), F32),
         ((a, q, own, span), BF16),
         ((a, q - 1, own, span), BF16),
@@ -636,12 +719,12 @@
         (12,),
         (a - 1,),
         (a - 1,),
-        (a - 1,),
-        (a - 1,),
+        (a, pieces, 2),
+        (a, pieces),
         (a, q - 1),
         (a, q - 1),
         (a - 1,),
-        (a - 1,),
+        (a,),
         (a - 1,),
         (a - 1,),
         (a, s - 1),

time: 62.7 us -> 69.4 us (1.11)
  Pallas kernels: 60.4 us -> 67.1 us
    pallas_call x1, Pallas kernels: 60.4 us -> 67.1 us  [on_device(): pl.pallas_call(functools.partial(layer_kernel, (a, s, p)), out_shape=jax....]
where the time goes in v4:
time: 69.4 us; the launch traced here: 69.2 us
  Pallas kernels  67.1 us (97%)
  local copies, waits for them, and re-layouts  1.47 us (2%)
    pallas_call x1, Pallas kernels, on_device(): pl.pallas_call(functools.partial(layer_kernel, (a, s, p)), out_shape=jax....  67.1 us
    unnamed x1, local copies, waits for them, and re-layouts  1.47 us

profile of v4, /device:TPU:0, one launch (start us, length us, event | category | flops | bytes accessed | tf_op | source)
XLA Modules:
  0.0 69.2 jit_solution(11009348571732536151)
XLA Ops:
  0.7 67.1 %shard_map.118 = bf16[16,2048]{1,0:T(8,128)(2,1)} custom-call(bf16[64,1024]{1,0:T(8,128)(2,1)} %q_hbm.1, bf16[2,1,128,256]{3,2,1,0:T(8,128)(2,1)} %kv_hbm.1, s32[1,2]{1,0:T(1,128)} %list_hbm.1, s32[1,1]{1,0:T(1,128)} %bitcast.4.len_hbm, bf16[16,2048]{1,0:T(8,128)(2,1)} %res_hbm.1, f32[1,2048]{1,0:T(1,128)} %bitcast.6, bf16[8,2048]{1,0:T(8,128)(2,1)} %bitcast.5, ...), custom_call_target="tpu_custom_call" | custom-call | tf_op jit(solution)/shard_map/pallas_call | solution.py:745
  67.8 1.5 %copy.15 = bf16[16,2048]{1,0:T(8,128)(2,1)} copy(bf16[16,2048]{1,0:T(8,128)(2,1)} %shard_map.118) | data formatting | bytes 131072

commit v5 on v3

--- a/solution.py
+++ b/solution.py
@@ -131,7 +131,7 @@
     wu_hbm,
     wd_hbm,
     out_ref,
-    q_ref,
+    q_all,
     res_ref,
     gain_ref,
     router_ref,
@@ -141,6 +141,7 @@
     wu,
     wd,
     kvbuf,
+    bias,
     att,
     part_f32,
     part,
@@ -162,8 +163,10 @@
     w_sem,
     kv_s,
     kv_r,
-    att_s,
-    att_r,
+    bias_s,
+    bias_r,
+    q_s,
+    q_r,
     rs_s,
     rs_r,
     mix_s,
@@ -191,7 +194,7 @@
     quarter = x * n_pair + c
     own = res_ref.shape[0]
     width = res_ref.shape[1]
-    group_rows, head_cols = q_ref.shape
+    group_rows, head_cols = q_hbm.shape
     local_heads = head_cols // HEAD_DIM
     kv_local = c * local_heads // (HEADS // KV_HEADS)
     blocks = kv_hbm.shape[1]
@@ -216,10 +219,10 @@
         pltpu.make_async_copy(src, dst, w_sem.at[i])
         for i, (src, dst) in enumerate(
             (
-                (q_hbm, q_ref),
-                (kv_hbm.at[kv_local], kvbuf.at[kv_slot]),
                 (list_hbm, list_ref),
                 (len_hbm, len_ref),
+                (kv_hbm.at[kv_local], kvbuf.at[kv_slot]),
+                (q_hbm, q_all.at[0]),
                 (wo_hbm, wo),
                 (res_hbm, res_ref),
                 (gain_hbm, gain_ref),
@@ -267,6 +270,27 @@
         )
         for d in range(1, n_attn)
     ]
+    q_copies = [None] + [
+        send(q_hbm, q_all.at[d], q_s.at[d - 1], q_r.at[d - 1], attn=ahead(d))
+        for d in range(1, n_attn)
+    ]
+    for load in loads[:2]:
+        load.wait()
+    block_keys = kvbuf.shape[1]
+    place = lax.broadcasted_iota(jnp.int32, bias.shape[1:], 1)
+    block, within = place // block_keys, place % block_keys
+    live = within < 0
+    for j in range(list_ref.shape[1]):
+        used = jnp.logical_and(
+            block == list_ref[0, j], within + j * block_keys < len_ref[0, 0]
+        )
+        live = jnp.logical_or(live, used)
+    bias[0] = jnp.where(live, 0.0, -jnp.inf)
+    bias_copies = [None] + [
+        send(bias.at[0], bias.at[d], bias_s.at[d - 1], bias_r.at[d - 1], attn=ahead(d))
+        for d in range(1, n_attn)
+    ]
+
     wd_copies = []
     for dx in range(1, n_sect):
         to_x = lax.rem(x + dx, n_sect)
@@ -279,35 +303,36 @@
                 sect=to_x,
             )
         )
-    for load in loads[:4]:
+    for load in loads[2:4]:
         load.wait()
     for copy in kv_copies:
         copy.wait_recv()
 
-    listed = list_ref.shape[1]
-    picked = [kvbuf[list_ref[0, j]] for j in range(listed)]
-    cache = jnp.concatenate(picked, axis=0)
+    cache = kvbuf[...].reshape(-1, kvbuf.shape[2])
     keys = cache[:, :HEAD_DIM]
     values = cache[:, HEAD_DIM:]
-    heads = jnp.concatenate(
-        [q_ref[:, h * HEAD_DIM : (h + 1) * HEAD_DIM] for h in range(local_heads)], axis=0
-    )
-    scores = lax.dot_general(
-        heads, keys, (((1,), (1,)), ((), ())), preferred_element_type=F32
-    ) / math.sqrt(HEAD_DIM)
-    place = lax.broadcasted_iota(jnp.int32, scores.shape, 1)
-    scores = jnp.where(place < len_ref[0, 0], scores, -jnp.inf)
-    lifted = jnp.exp(scores - jnp.max(scores, axis=-1, keepdims=True))
-    row_total = jnp.sum(lifted, axis=-1, keepdims=True)
-    mixed = jnp.dot(lifted.astype(BF16), values, preferred_element_type=F32) / row_total
-    for h in range(local_heads):
-        att[0, :, h * HEAD_DIM : (h + 1) * HEAD_DIM] = mixed[
-            h * group_rows : (h + 1) * group_rows
-        ].astype(BF16)
-    att_copies = [None] + [
-        send(att.at[0], att.at[d], att_s.at[d - 1], att_r.at[d - 1], attn=ahead(d))
-        for d in range(1, n_attn)
-    ]
+    scale = 1.0 / math.sqrt(HEAD_DIM)
+    stacked = local_heads // (2 - local_heads % 2)
+
+    def attend(d):
+        if d:
+            q_copies[d].wait_recv()
+            bias_copies[d].wait_recv()
+        for first in range(0, local_heads, stacked):
+            spans = [
+                slice((first + h) * HEAD_DIM, (first + h + 1) * HEAD_DIM) for h in range(stacked)
+            ]
+            heads = jnp.concatenate([q_all[d, :, span] for span in spans], axis=0)
+            scores = lax.dot_general(
+                heads, keys, (((1,), (1,)), ((), ())), preferred_element_type=F32
+            )
+            scores = scores * scale + bias[d]
+            lifted = jnp.exp(scores - jnp.max(scores, axis=-1, keepdims=True))
+            row_total = jnp.sum(lifted, axis=-1, keepdims=True)
+            mixed = jnp.dot(lifted.astype(BF16), values, preferred_element_type=F32)
+            mixed = (mixed / row_total).astype(BF16)
+            for h in range(stacked):
+                att[d, :, spans[h]] = mixed[h * group_rows : (h + 1) * group_rows]
 
     def plane(step):
         return lax.div(step, n_pair), lax.rem(step, n_pair)
@@ -317,8 +342,7 @@
     mix_copies = []
 
     def project(d):
-        if d:
-            att_copies[d].wait_recv()
+        attend(d)
         value = jnp.dot(att[d], wo[...], preferred_element_type=F32)
         value = value.reshape(part_f32.shape[1:])
         part_f32[d] = value
@@ -575,7 +599,7 @@
     key_rows, key_cols = kv_pool.shape[2:]
     wide = width + LANES
     buffers = [
-        ((group_rows, head_cols), BF16),
+        ((a, group_rows, head_cols), BF16),
         ((own, width), BF16),
         ((1, width), F32),
         (router.shape[::-1], BF16),
@@ -585,6 +609,7 @@
         ((width, hidden_part), BF16),
         ((s, hidden_part, out_cols), BF16),
         ((a * kv_pool.shape[1], key_rows, key_cols), BF16),
+        ((a, 1, a * kv_pool.shape[1] * key_rows), F32),
         ((a, group_rows, head_cols), BF16),
         ((a, q, own, span), F32),
         ((a, q, own, span), BF16),
@@ -638,6 +663,8 @@
         (a - 1,),
         (a - 1,),
         (a - 1,),
+        (a - 1,),
+        (a - 1,),
         (a, q - 1),
         (a, q - 1),
         (a - 1,),

time: 62.7 us -> 64.5 us (1.029)
  Pallas kernels: 60.4 us -> 62.2 us
    pallas_call x1, Pallas kernels: 60.4 us -> 62.2 us  [on_device(): pl.pallas_call(functools.partial(layer_kernel, (a, s, p)), out_shape=jax....]
where the time goes in v5:
time: 64.5 us; the launch traced here: 64.3 us
  Pallas kernels  62.2 us (96%)
  local copies, waits for them, and re-layouts  1.47 us (2%)
  between operations  0.66 us (1%)
    pallas_call x1, Pallas kernels, on_device(): pl.pallas_call(functools.partial(layer_kernel, (a, s, p)), out_shape=jax....  62.2 us
    unnamed x1, local copies, waits for them, and re-layouts  1.47 us

profile of v5, /device:TPU:0, one launch (start us, length us, event | category | flops | bytes accessed | tf_op | source)
XLA Modules:
  0.0 64.3 jit_solution(14160409164739196481)
XLA Ops:
  0.7 62.2 %shard_map.118 = bf16[16,2048]{1,0:T(8,128)(2,1)} custom-call(bf16[64,1024]{1,0:T(8,128)(2,1)} %q_hbm.1, bf16[2,1,128,256]{3,2,1,0:T(8,128)(2,1)} %kv_hbm.1, s32[1,2]{1,0:T(1,128)} %list_hbm.1, s32[1,1]{1,0:T(1,128)} %bitcast.4.len_hbm, bf16[16,2048]{1,0:T(8,128)(2,1)} %res_hbm.1, f32[1,2048]{1,0:T(1,128)} %bitcast.6, bf16[8,2048]{1,0:T(8,128)(2,1)} %bitcast.5, ...), custom_call_target="tpu_custom_call" | custom-call | tf_op jit(solution)/shard_map/pallas_call | solution.py:689
  62.8 1.5 %copy.15 = bf16[16,2048]{1,0:T(8,128)(2,1)} copy(bf16[16,2048]{1,0:T(8,128)(2,1)} %shard_map.118) | data formatting | bytes 131072

commit v6 on v3

--- a/solution.py
+++ b/solution.py
@@ -142,10 +142,8 @@
     wd,
     kvbuf,
     att,
-    part_f32,
     part,
-    rs_in,
-    sum_out,
+    mix_own,
     mix_in,
     mix_f32,
     rows,
@@ -164,8 +162,6 @@
     kv_r,
     att_s,
     att_r,
-    rs_s,
-    rs_r,
     mix_s,
     mix_r,
     nz_s,
@@ -294,7 +290,7 @@
     )
     scores = lax.dot_general(
         heads, keys, (((1,), (1,)), ((), ())), preferred_element_type=F32
-    ) / math.sqrt(HEAD_DIM)
+    ) * (1.0 / math.sqrt(HEAD_DIM))
     place = lax.broadcasted_iota(jnp.int32, scores.shape, 1)
     scores = jnp.where(place < len_ref[0, 0], scores, -jnp.inf)
     lifted = jnp.exp(scores - jnp.max(scores, axis=-1, keepdims=True))
@@ -313,61 +309,46 @@
         return lax.div(step, n_pair), lax.rem(step, n_pair)
 
     loads[4].wait()
-    rs_copies = []
-    mix_copies = []
-
-    def project(d):
+    for d in range(n_attn):
         if d:
             att_copies[d].wait_recv()
         value = jnp.dot(att[d], wo[...], preferred_element_type=F32)
-        value = value.reshape(part_f32.shape[1:])
-        part_f32[d] = value
+        value = value.reshape(part.shape[1:])
         part[d] = value.astype(BF16)
-        copies = []
-        for j in range(1, quarters):
+        if d == 0:
+            mix_own[...] = value
+        for j in range(quarters):
+            if d + j == 0:
+                continue
             to = lax.rem(quarter + j, quarters)
             to_x, to_c = plane(to)
-            copies.append(
-                send(
-                    part.at[d, to],
-                    rs_in.at[d, j - 1],
-                    rs_s.at[d, j - 1],
-                    rs_r.at[d, j - 1],
-                    sect=to_x,
-                    pair=to_c,
-                )
+            send(
+                part.at[d, to],
+                mix_in.at[z, j],
+                mix_s.at[d, j],
+                mix_r.at[z, j],
+                attn=behind(d),
+                sect=to_x,
+                pair=to_c,
             )
-        rs_copies.append(copies)
-
-    def pass_on(d):
-        for copy in rs_copies[d]:
-            copy.wait_recv()
-        total = part_f32[d, quarter]
-        for j in range(quarters - 1):
-            total = total + rs_in[d, j].astype(F32)
-        if d == 0:
-            mix_f32[z] = total
-        else:
-            sum_out[d - 1] = total.astype(BF16)
-            mix_copies.append(
-                send(
-                    sum_out.at[d - 1],
-                    mix_in.at[z],
-                    mix_s.at[d - 1],
-                    mix_r.at[d - 1],
-                    attn=behind(d),
-                )
-            )
-
-    for d in range(n_attn + 1):
-        if d < n_attn:
-            project(d)
-        if d:
-            pass_on(d - 1)
-    for d in range(1, n_attn):
-        mix_copies[d - 1].wait_recv()
-        mix_f32[ahead(d)] = mix_in[ahead(d)].astype(F32)
-
+    for d in range(n_attn):
+        src = ahead(d)
+        total = None
+        for j in range(quarters):
+            if d + j == 0:
+                total = mix_own[quarter]
+                continue
+            pltpu.make_async_remote_copy(
+                src_ref=part.at[d, j],
+                dst_ref=mix_in.at[src, j],
+                send_sem=mix_s.at[d, j],
+                recv_sem=mix_r.at[src, j],
+                device_id={"attn": ahead(1)},
+                device_id_type=MESH,
+            ).wait_recv()
+            got = mix_in[src, j].astype(F32)
+            total = got if total is None else total + got
+        mix_f32[src] = total
     for load in loads[5:9]:
         load.wait()
 
@@ -586,11 +567,9 @@
         ((s, hidden_part, out_cols), BF16),
         ((a * kv_pool.shape[1], key_rows, key_cols), BF16),
         ((a, group_rows, head_cols), BF16),
-        ((a, q, own, span), F32),
         ((a, q, own, span), BF16),
-        ((a, q - 1, own, span), BF16),
-        ((a - 1, own, span), BF16),
-        ((a, own, span), BF16),
+        ((q, own, span), F32),
+        ((a, q, own, span), BF16),
         ((a, own, span), F32),
         ((a, q, own, wide), BF16),
         ((a, p, s, own, width), F32),
@@ -638,10 +617,8 @@
         (a - 1,),
         (a - 1,),
         (a - 1,),
-        (a, q - 1),
-        (a, q - 1),
-        (a - 1,),
-        (a - 1,),
+        (a, q),
+        (a, q),
         (a - 1,),
         (a - 1,),
         (a, s - 1),

time: 62.7 us -> 63.8 us (1.018)
  Pallas kernels: 60.4 us -> 61.5 us
    pallas_call x1, Pallas kernels: 60.4 us -> 61.5 us  [on_device(): pl.pallas_call(functools.partial(layer_kernel, (a, s, p)), out_shape=jax....]
where the time goes in v6:
time: 63.8 us; the launch traced here: 63.6 us
  Pallas kernels  61.5 us (96%)
  local copies, waits for them, and re-layouts  1.47 us (2%)
  between operations  0.66 us (1%)
    pallas_call x1, Pallas kernels, on_device(): pl.pallas_call(functools.partial(layer_kernel, (a, s, p)), out_shape=jax....  61.5 us
    unnamed x1, local copies, waits for them, and re-layouts  1.47 us

profile of v6, /device:TPU:0, one launch (start us, length us, event | category | flops | bytes accessed | tf_op | source)
XLA Modules:
  0.0 63.6 jit_solution(15742519999117049362)
XLA Ops:
  0.7 61.5 %shard_map.118 = bf16[16,2048]{1,0:T(8,128)(2,1)} custom-call(bf16[64,1024]{1,0:T(8,128)(2,1)} %q_hbm.1, bf16[2,1,128,256]{3,2,1,0:T(8,128)(2,1)} %kv_hbm.1, s32[1,2]{1,0:T(1,128)} %list_hbm.1, s32[1,1]{1,0:T(1,128)} %bitcast.4.len_hbm, bf16[16,2048]{1,0:T(8,128)(2,1)} %res_hbm.1, f32[1,2048]{1,0:T(1,128)} %bitcast.6, bf16[8,2048]{1,0:T(8,128)(2,1)} %bitcast.5, ...), custom_call_target="tpu_custom_call" | custom-call | tf_op jit(solution)/shard_map/pallas_call | solution.py:639
  62.1 1.5 %copy.15 = bf16[16,2048]{1,0:T(8,128)(2,1)} copy(bf16[16,2048]{1,0:T(8,128)(2,1)} %shard_map.118) | data formatting | bytes 131072

commit v7 on v3

--- a/solution.py
+++ b/solution.py
@@ -289,25 +289,40 @@
     cache = jnp.concatenate(picked, axis=0)
     keys = cache[:, :HEAD_DIM]
     values = cache[:, HEAD_DIM:]
-    heads = jnp.concatenate(
-        [q_ref[:, h * HEAD_DIM : (h + 1) * HEAD_DIM] for h in range(local_heads)], axis=0
-    )
-    scores = lax.dot_general(
-        heads, keys, (((1,), (1,)), ((), ())), preferred_element_type=F32
-    ) / math.sqrt(HEAD_DIM)
-    place = lax.broadcasted_iota(jnp.int32, scores.shape, 1)
-    scores = jnp.where(place < len_ref[0, 0], scores, -jnp.inf)
-    lifted = jnp.exp(scores - jnp.max(scores, axis=-1, keepdims=True))
-    row_total = jnp.sum(lifted, axis=-1, keepdims=True)
-    mixed = jnp.dot(lifted.astype(BF16), values, preferred_element_type=F32) / row_total
-    for h in range(local_heads):
-        att[0, :, h * HEAD_DIM : (h + 1) * HEAD_DIM] = mixed[
-            h * group_rows : (h + 1) * group_rows
-        ].astype(BF16)
-    att_copies = [None] + [
-        send(att.at[0], att.at[d], att_s.at[d - 1], att_r.at[d - 1], attn=ahead(d))
-        for d in range(1, n_attn)
-    ]
+    pieces, piece_cols = att.shape[1], att.shape[3]
+    piece_heads = piece_cols // HEAD_DIM
+    att_copies = [[] for _ in range(n_attn)]
+    for piece in range(pieces):
+        start = piece * piece_cols
+        heads = jnp.concatenate(
+            [
+                q_ref[:, start + h * HEAD_DIM : start + (h + 1) * HEAD_DIM]
+                for h in range(piece_heads)
+            ],
+            axis=0,
+        )
+        scores = lax.dot_general(
+            heads, keys, (((1,), (1,)), ((), ())), preferred_element_type=F32
+        ) * (1.0 / math.sqrt(HEAD_DIM))
+        place = lax.broadcasted_iota(jnp.int32, scores.shape, 1)
+        scores = jnp.where(place < len_ref[0, 0], scores, -jnp.inf)
+        lifted = jnp.exp(scores - jnp.max(scores, axis=-1, keepdims=True))
+        row_total = jnp.sum(lifted, axis=-1, keepdims=True)
+        mixed = jnp.dot(lifted.astype(BF16), values, preferred_element_type=F32) / row_total
+        for h in range(piece_heads):
+            att[0, piece, :, h * HEAD_DIM : (h + 1) * HEAD_DIM] = mixed[
+                h * group_rows : (h + 1) * group_rows
+            ].astype(BF16)
+        for d in range(1, n_attn):
+            att_copies[d].append(
+                send(
+                    att.at[0, piece],
+                    att.at[d, piece],
+                    att_s.at[d - 1, piece],
+                    att_r.at[d - 1, piece],
+                    attn=ahead(d),
+                )
+            )
 
     def plane(step):
         return lax.div(step, n_pair), lax.rem(step, n_pair)
@@ -317,9 +332,15 @@
     mix_copies = []
 
     def project(d):
-        if d:
-            att_copies[d].wait_recv()
-        value = jnp.dot(att[d], wo[...], preferred_element_type=F32)
+        for copy in att_copies[d]:
+            copy.wait_recv()
+        value = jnp.dot(att[d, 0], wo[:piece_cols], preferred_element_type=F32)
+        for piece in range(1, pieces):
+            value += jnp.dot(
+                att[d, piece],
+                wo[piece * piece_cols : (piece + 1) * piece_cols],
+                preferred_element_type=F32,
+            )
         value = value.reshape(part_f32.shape[1:])
         part_f32[d] = value
         part[d] = value.astype(BF16)
@@ -524,23 +545,25 @@
     spread(0)
     spread_on(0)
     up(0)
-    turns = list(range(1, n_attn)) + [0]
     early = max(0, n_attn - 3)
     for d in range(1, n_attn):
         spread(d)
-        if d >= 2:
+        if d == 1:
+            to_sect(0)
+        else:
             spread_on(d - 1)
             up(d - 1)
         if d >= 3:
             to_sect(d - 2)
     spread_on(n_attn - 1)
     up(n_attn - 1)
-    for i in range(early - 1):
-        give_back(turns[i])
-    for i in range(early, n_attn):
-        to_sect(turns[i])
-        if i:
-            give_back(turns[i - 1])
+    for d in range(1, early):
+        give_back(d)
+    for d in range(early + 1, n_attn):
+        to_sect(d)
+        if d > 1:
+            give_back(d - 1)
+    give_back(n_attn - 1)
     joined = give_back(0)
     for d in range(1, n_attn):
         ret_copies[d].wait_recv()
@@ -574,6 +597,7 @@
     out_cols = w_down.shape[2]
     key_rows, key_cols = kv_pool.shape[2:]
     wide = width + LANES
+    pieces = 2 - head_cols // HEAD_DIM % 2
     buffers = [
         ((group_rows, head_cols), BF16),
         ((own, width), BF16),
@@ -585,7 +609,7 @@
         ((width, hidden_part), BF16),
         ((s, hidden_part, out_cols), BF16),
         ((a * kv_pool.shape[1], key_rows, key_cols), BF16),
-        ((a, group_rows, head_cols), BF16),
+        ((a, pieces, group_rows, head_cols // pieces), BF16),
         ((a, q, own, span), F32),
         ((a, q, own, span), BF16),
         ((a, q - 1, own, span), BF16),
@@ -636,8 +660,8 @@
         (12,),
         (a - 1,),
         (a - 1,),
-        (a - 1,),
-        (a - 1,),
+        (a - 1, pieces),
+        (a - 1, pieces),
         (a, q - 1),
         (a, q - 1),
         (a - 1,),

time: 62.7 us -> 63.5 us (1.013)
  Pallas kernels: 60.4 us -> 61.2 us
    pallas_call x1, Pallas kernels: 60.4 us -> 61.2 us  [on_device(): pl.pallas_call(functools.partial(layer_kernel, (a, s, p)), out_shape=jax....]
where the time goes in v7:
time: 63.5 us; the launch traced here: 63.4 us
  Pallas kernels  61.2 us (96%)
  local copies, waits for them, and re-layouts  1.47 us (2%)
  between operations  0.66 us (1%)
    pallas_call x1, Pallas kernels, on_device(): pl.pallas_call(functools.partial(layer_kernel, (a, s, p)), out_shape=jax....  61.2 us
    unnamed x1, local copies, waits for them, and re-layouts  1.47 us

profile of v7, /device:TPU:0, one launch (start us, length us, event | category | flops | bytes accessed | tf_op | source)
XLA Modules:
  0.0 63.4 jit_solution(17449556264640564728)
XLA Ops:
  0.7 61.2 %shard_map.118 = bf16[16,2048]{1,0:T(8,128)(2,1)} custom-call(bf16[64,1024]{1,0:T(8,128)(2,1)} %q_hbm.1, bf16[2,1,128,256]{3,2,1,0:T(8,128)(2,1)} %kv_hbm.1, s32[1,2]{1,0:T(1,128)} %list_hbm.1, s32[1,1]{1,0:T(1,128)} %bitcast.4.len_hbm, bf16[16,2048]{1,0:T(8,128)(2,1)} %res_hbm.1, f32[1,2048]{1,0:T(1,128)} %bitcast.6, bf16[8,2048]{1,0:T(8,128)(2,1)} %bitcast.5, ...), custom_call_target="tpu_custom_call" | custom-call | tf_op jit(solution)/shard_map/pallas_call | solution.py:686
  61.9 1.5 %copy.15 = bf16[16,2048]{1,0:T(8,128)(2,1)} copy(bf16[16,2048]{1,0:T(8,128)(2,1)} %shard_map.118) | data formatting | bytes 131072

commit v8 on v3

--- a/solution.py
+++ b/solution.py
@@ -238,7 +238,7 @@
     for dz in range(n_attn):
         for dx in range(n_sect):
             for dc in range(n_pair):
-                if dz + dx + dc:
+                if (dz == 0) != (dx + dc == 0):
                     pl.semaphore_signal(
                         barrier,
                         inc=1,
@@ -249,7 +249,7 @@
                         },
                         device_id_type=MESH,
                     )
-    pl.semaphore_wait(barrier, n_attn * quarters - 1)
+    pl.semaphore_wait(barrier, n_attn + quarters - 2)
 
     def ahead(d):
         return lax.rem(z + d, n_attn)
@@ -294,7 +294,7 @@
     )
     scores = lax.dot_general(
         heads, keys, (((1,), (1,)), ((), ())), preferred_element_type=F32
-    ) / math.sqrt(HEAD_DIM)
+    ) * (1.0 / math.sqrt(HEAD_DIM))
     place = lax.broadcasted_iota(jnp.int32, scores.shape, 1)
     scores = jnp.where(place < len_ref[0, 0], scores, -jnp.inf)
     lifted = jnp.exp(scores - jnp.max(scores, axis=-1, keepdims=True))

time: 62.7 us -> 61.3 us (0.978)
  Pallas kernels: 60.4 us -> 59 us
    pallas_call x1, Pallas kernels: 60.4 us -> 59 us  [on_device(): pl.pallas_call(functools.partial(layer_kernel, (a, s, p)), out_shape=jax....]
where the time goes in v8:
time: 61.3 us; the launch traced here: 61.2 us
  Pallas kernels  59 us (96%)
  local copies, waits for them, and re-layouts  1.47 us (2%)
  between operations  0.66 us (1%)
    pallas_call x1, Pallas kernels, on_device(): pl.pallas_call(functools.partial(layer_kernel, (a, s, p)), out_shape=jax....  59 us
    unnamed x1, local copies, waits for them, and re-layouts  1.47 us

profile of v8, /device:TPU:0, one launch (start us, length us, event | category | flops | bytes accessed | tf_op | source)
XLA Modules:
  0.0 61.2 jit_solution(6756810543453552621)
XLA Ops:
  0.7 59.0 %shard_map.118 = bf16[16,2048]{1,0:T(8,128)(2,1)} custom-call(bf16[64,1024]{1,0:T(8,128)(2,1)} %q_hbm.1, bf16[2,1,128,256]{3,2,1,0:T(8,128)(2,1)} %kv_hbm.1, s32[1,2]{1,0:T(1,128)} %list_hbm.1, s32[1,1]{1,0:T(1,128)} %bitcast.4.len_hbm, bf16[16,2048]{1,0:T(8,128)(2,1)} %res_hbm.1, f32[1,2048]{1,0:T(1,128)} %bitcast.6, bf16[8,2048]{1,0:T(8,128)(2,1)} %bitcast.5, ...), custom_call_target="tpu_custom_call" | custom-call | tf_op jit(solution)/shard_map/pallas_call | solution.py:662
  59.7 1.5 %copy.15 = bf16[16,2048]{1,0:T(8,128)(2,1)} copy(bf16[16,2048]{1,0:T(8,128)(2,1)} %shard_map.118) | data formatting | bytes 131072

commit v9 on v8

--- a/solution.py
+++ b/solution.py
@@ -397,13 +397,13 @@
     route = jnp.transpose(
         jnp.concatenate([route, jnp.zeros((LANES, LANES - own), F32)], axis=1)
     )[:own]
-    rows[0, quarter, :, :width] = normed
-    rows[0, quarter, :, width:] = route.astype(BF16)
+    rows[0, c, x, :, :width] = normed
+    rows[0, c, x, :, width:] = route.astype(BF16)
 
     nz_copies = [None] + [
         send(
-            rows.at[0, quarter],
-            rows.at[d, quarter],
+            rows.at[0, c, x],
+            rows.at[d, c, x],
             nz_s.at[d - 1],
             nz_r.at[d - 1],
             attn=ahead(d),
@@ -417,38 +417,33 @@
     for copy in wd_copies:
         copy.wait_recv()
 
-    def to_cores(d, dx):
-        from_q = lax.rem(x + (n_sect - dx), n_sect) * n_pair + c
-        return [
-            send(
-                rows.at[d, from_q],
-                rows.at[d, from_q],
-                nc_s.at[d, dx, dc - 1],
-                nc_r.at[d, dx, dc - 1],
-                pair=lax.rem(c + dc, n_pair),
-            )
-            for dc in range(1, n_pair)
-        ]
-
     def spread(d):
         if d:
             nz_copies[d].wait_recv()
         nx_copies[d] = [
             send(
-                rows.at[d, quarter],
-                rows.at[d, quarter],
+                rows.at[d, c, x],
+                rows.at[d, c, x],
                 nx_s.at[d, dx - 1],
                 nx_r.at[d, dx - 1],
                 sect=lax.rem(x + dx, n_sect),
             )
             for dx in range(1, n_sect)
         ]
-        nc_copies[d] = to_cores(d, 0)
 
     def spread_on(d):
-        for dx in range(1, n_sect):
-            nx_copies[d][dx - 1].wait_recv()
-            nc_copies[d] += to_cores(d, dx)
+        for copy in nx_copies[d]:
+            copy.wait_recv()
+        nc_copies[d] = [
+            send(
+                rows.at[d, c],
+                rows.at[d, c],
+                nc_s.at[d, dc - 1],
+                nc_r.at[d, dc - 1],
+                pair=lax.rem(c + dc, n_pair),
+            )
+            for dc in range(1, n_pair)
+        ]
 
     sect_copies = [None] * n_attn
     pair_copies = [None] * n_attn
@@ -469,11 +464,9 @@
         weights = rows[d].reshape(quarters * own, rows.shape[-1])[:, width:].astype(F32)
         lanes = lax.broadcasted_iota(jnp.int32, weights.shape, 1)
         weight = jnp.sum(jnp.where(lanes == expert, weights, 0.0), axis=-1, keepdims=True)
-        value = (value * weight).reshape(n_sect, n_pair, own, value.shape[-1])
-        for i in range(n_sect):
-            for j in range(n_pair):
-                prod_f32[d, j, i] = value[i, j]
-                prod[d, j, i] = value[i, j].astype(BF16)
+        value = (value * weight).reshape(n_pair, n_sect, own, value.shape[-1])
+        prod_f32[d] = value
+        prod[d] = value.astype(BF16)
         pair_copies[d] = [
             send(
                 prod.at[d, lax.rem(c + dc, n_pair)],
@@ -592,7 +585,7 @@
         ((a - 1, own, span), BF16),
         ((a, own, span), BF16),
         ((a, own, span), F32),
-        ((a, q, own, wide), BF16),
+        ((a, p, s, own, wide), BF16),
         ((a, p, s, own, width), F32),
         ((a, p, s, own, width), BF16),
         ((a, p - 1, s, own, width), BF16),
@@ -646,8 +639,8 @@
         (a - 1,),
         (a, s - 1),
         (a, s - 1),
-        (a, s, p - 1),
-        (a, s, p - 1),
+        (a, p - 1),
+        (a, p - 1),
         (s - 1,),
         (s - 1,),
         (a, p - 1),

time: 61.3 us -> 61.4 us (level)
  no operation moved by 1% of the time
where the time goes in v9:
time: 61.4 us; the launch traced here: 61.3 us
  Pallas kernels  59.1 us (96%)
  local copies, waits for them, and re-layouts  1.47 us (2%)
  between operations  0.66 us (1%)
    pallas_call x1, Pallas kernels, on_device(): pl.pallas_call(functools.partial(layer_kernel, (a, s, p)), out_shape=jax....  59.1 us
    unnamed x1, local copies, waits for them, and re-layouts  1.47 us

profile of v9, /device:TPU:0, one launch (start us, length us, event | category | flops | bytes accessed | tf_op | source)
XLA Modules:
  0.0 61.3 jit_solution(11830175902909616337)
XLA Ops:
  0.7 59.1 %shard_map.118 = bf16[16,2048]{1,0:T(8,128)(2,1)} custom-call(bf16[64,1024]{1,0:T(8,128)(2,1)} %q_hbm.1, bf16[2,1,128,256]{3,2,1,0:T(8,128)(2,1)} %kv_hbm.1, s32[1,2]{1,0:T(1,128)} %list_hbm.1, s32[1,1]{1,0:T(1,128)} %bitcast.4.len_hbm, bf16[16,2048]{1,0:T(8,128)(2,1)} %res_hbm.1, f32[1,2048]{1,0:T(1,128)} %bitcast.6, bf16[8,2048]{1,0:T(8,128)(2,1)} %bitcast.5, ...), custom_call_target="tpu_custom_call" | custom-call | tf_op jit(solution)/shard_map/pallas_call | solution.py:655
  59.8 1.5 %copy.15 = bf16[16,2048]{1,0:T(8,128)(2,1)} copy(bf16[16,2048]{1,0:T(8,128)(2,1)} %shard_map.118) | data formatting | bytes 131072
